TPU v7x, 256 devices: a whole 4x4x8 slice. The times are simulated.
256 devices in a mesh: gx: 16 (over y, x), gy: 16 (over z, core).
Axes of the slice: x: 4, y: 4, z: 8, core: 2. Of those that a mesh axis runs over, the one named last changes fastest.
Arguments:
- pressure: float32 [2, 2048, 2048], P(None, 'gx', 'gy'), may hold values from 0.5 to 1.5
- saturations: float32 [2, 2, 2048, 2048], P(None, None, 'gx', 'gy'), may hold values from 0.05 to 0.4
- old_mass: float32 [3, 2, 2048, 2048], P(None, None, 'gx', 'gy'), may hold values from 0 to 0.4
- pore_volume: float32 [2, 2048, 2048], P(None, 'gx', 'gy'), may hold values from 0.3 to 3
- transmissibility: float32 [3, 2, 2048, 2048], P(None, None, 'gx', 'gy'), may hold values from 0.3 to 3
- direction: float32 [3, 2, 2048, 2048], P(None, None, 'gx', 'gy'), may hold values from -6 to 6
- seg_pressure: float32 [512, 128], P('gx'), may hold values from 0.4 to 1.2
- seg_direction: float32 [512, 128], P('gx'), may hold values from -6 to 6
- perf_cell: int32 [512, 128], P('gx'), may hold values from 0 to 524287, as said below
- well_index: float32 [512, 128], P('gx'), may hold values from 0.2 to 2
- parent: int32 [512, 128], P('gx'), may hold values from 0 to 126, as said below
- seg_head: float32 [512, 128], P('gx'), may hold values from 0 to 0.3
- well_mode: int32 [512], P('gx'), may hold values from 0 to 1
- bhp_limit: float32 [512], P('gx'), may hold values from 0.3 to 0.8
- guide_rate: float32 [512], P('gx'), may hold values from 0.5 to 5
- group_of: int32 [512, 1], P('gx'), may hold values from 0 to 127
- group_target: float32 [128], replicated, may hold values from 200 to 800
Outputs:
- cell_residual: float32 [3, 2, 2048, 2048], P(None, None, 'gx', 'gy')
- cell_jvp: float32 [3, 2, 2048, 2048], P(None, None, 'gx', 'gy')
- seg_residual: float32 [512, 128], P(('gx', 'gy'))
- seg_jvp: float32 [512, 128], P(('gx', 'gy'))
- group_rates: float32 [3, 128], replicated
Inputs may be any that keep to these rules, and one draw needn't show every extreme that they name: perf_cell codes (layer * 128 + xl) * 2048 + row, with xl the column within the strip of 128 columns of the well's block of 32 wells. `parent`: segment 0 of every well names itself; every other segment names a segment of lower number. `group_of`: every group has at least one well.
All inputs are finite; a program needn't handle non-finite values.
Results may differ from a plain program's by a relative error of at most 0.0003.
Values sent between devices are 32-bit elements; how exact they have to be, the bound alone decides.
A program may use at most 128 MiB of HBM per device.

v0:
```python
import jax
import jax.numpy as jnp
from jax import lax
from jax.sharding import PartitionSpec as P

COMPRESS = (0.05, 0.2, 1.0)
VISCOSITY = (0.5, 1.0, 0.2)
DENSITY = (1.0, 0.8, 0.2)
ROCK_COMP = 0.01
GRAVITY = 0.05
UPWIND_WIDTH = 0.02
FRICTION = 0.002
RATE_SCALE = 0.1


def padded_2(x, sides, width):
    for axis, dim in sides:
        devices, length = (lax.axis_size(axis), x.shape[dim])
        up = [(i, (i + 1) % devices) for i in range(devices - 1)]
        down = [(j, i) for i, j in up]
        last = lax.slice_in_dim(x, length - width, length, axis=dim)
        first = lax.slice_in_dim(x, 0, width, axis=dim)
        before = lax.ppermute(last, axis, up)
        after = lax.ppermute(first, axis, down)
        x = jnp.concatenate([before, x, after], axis=dim)
    return x


def phase_props(press, water, gas):
    oil = 1.0 - water - gas
    satur = (water, oil, gas)
    rock = 1.0 + ROCK_COMP * (press - 1.0)
    mobility = []
    masses = []
    for phase in range(3):
        volume = jnp.exp(COMPRESS[phase] * (press - 1.0))
        mobility.append(satur[phase] * satur[phase] * volume / VISCOSITY[phase])
        masses.append(rock * satur[phase] * volume)
    return (jnp.stack(mobility), jnp.stack(masses))


def face_flux(press_in, press_out, mobil_in, mobil_out, trans, lift):
    fluxes = []
    for phase in range(3):
        potential = press_in - press_out + DENSITY[phase] * lift
        upwind = jax.nn.sigmoid(potential / UPWIND_WIDTH)
        fluxes.append(
            trans * (upwind * mobil_in[phase] + (1.0 - upwind) * mobil_out[phase]) * potential
        )
    return jnp.stack(fluxes)


def ancestry(parent):
    count = parent.shape[1]
    segment_ids = jnp.arange(count, dtype=jnp.int32)
    reach = (segment_ids[None, :, None] == segment_ids[None, None, :]) | (
        parent[:, None, :] == segment_ids[None, :, None]
    )
    reach = reach.astype(jnp.bfloat16)
    for level in range((count - 1).bit_length()):
        product = jnp.einsum("wsu,wut->wst", reach, reach, preferred_element_type=jnp.float32)
        reach = jnp.minimum(product, 1.0).astype(jnp.bfloat16)
    return reach.astype(jnp.float32)


def segment_terms(parent, seg_head, well_mode, bhp_limit, target):
    reach = ancestry(parent)

    def equations(total_vals, seg_vals):
        flow = jnp.einsum("wst,wt->ws", reach, total_vals, precision=lax.Precision.HIGHEST)
        above = jnp.take_along_axis(seg_vals, parent, axis=1)
        inner = seg_vals - above - seg_head - FRICTION * flow
        root = jnp.where(
            well_mode == 1, RATE_SCALE * (flow[:, 0] - target), seg_vals[:, 0] - bhp_limit
        )
        return inner.at[:, 0].set(root)

    return equations


def per_device(
    pressure,
    saturations,
    old_mass,
    pore_volume,
    transmissibility,
    direction,
    seg_pressure,
    seg_direction,
    perf_cell,
    well_index,
    parent,
    seg_head,
    well_mode,
    bhp_limit,
    guide_rate,
    group_of,
    group_target,
):
    layers, cols, rows = pressure.shape
    col_count = lax.axis_size("gx")
    row_count = lax.axis_size("gy")
    col_index = lax.axis_index("gx")
    row_index = lax.axis_index("gy")
    col_glob = col_index * cols + jnp.arange(cols, dtype=jnp.int32)
    row_glob = row_index * rows + jnp.arange(rows, dtype=jnp.int32)
    trans_cols = jnp.where(
        (col_glob == cols * col_count - 1)[None, :, None], 0.0, transmissibility[0]
    )
    trans_rows = jnp.where(
        (row_glob == rows * row_count - 1)[None, None, :], 0.0, transmissibility[1]
    )
    stacked = jnp.concatenate(
        [pressure[None], saturations, direction, trans_cols[None], trans_rows[None]], axis=0
    )
    padded = padded_2(stacked, (("gx", 2), ("gy", 3)), 1)
    state_pad = padded[0:3]
    direc_pad = padded[3:6]
    tcol_pad = padded[6]
    trow_pad = padded[7]
    all_rows = rows * row_count
    layer_span = cols * all_rows
    layer = perf_cell // layer_span
    remain = perf_cell % layer_span
    local_row = remain % all_rows - row_index * rows
    owned = (local_row >= 0) & (local_row < rows)
    flat_cell = (layer * cols + remain // all_rows) * rows + jnp.clip(local_row, 0, rows - 1)
    weight = jnp.where(owned, well_index, 0.0)

    def local_terms(state, seg_vals):
        press = state[0]
        mobility, masses = phase_props(press, state[1], state[2])
        mobil_in = mobility[:, :, 1:-1, 1:-1]
        press_in = press[:, 1:-1, 1:-1]
        residual = masses[:, :, 1:-1, 1:-1] * pore_volume - old_mass
        flux_cols = face_flux(
            press[:, :-1, 1:-1],
            press[:, 1:, 1:-1],
            mobility[:, :, :-1, 1:-1],
            mobility[:, :, 1:, 1:-1],
            tcol_pad[:, :-1, 1:-1],
            0.0,
        )
        residual = residual + flux_cols[:, :, 1:] - flux_cols[:, :, :-1]
        flux_rows = face_flux(
            press[:, 1:-1, :-1],
            press[:, 1:-1, 1:],
            mobility[:, :, 1:-1, :-1],
            mobility[:, :, 1:-1, 1:],
            trow_pad[:, 1:-1, :-1],
            0.0,
        )
        residual = residual + flux_rows[:, :, :, 1:] - flux_rows[:, :, :, :-1]
        flux_layers = face_flux(
            press_in[:-1],
            press_in[1:],
            mobil_in[:, :-1],
            mobil_in[:, 1:],
            transmissibility[2][:-1],
            GRAVITY,
        )
        residual = (
            residual
            + jnp.pad(flux_layers, ((0, 0), (0, 1), (0, 0), (0, 0)))
            - jnp.pad(flux_layers, ((0, 0), (1, 0), (0, 0), (0, 0)))
        )
        mobil_flat = mobil_in.reshape(3, -1)
        rates = weight * mobil_flat[:, flat_cell] * (press_in.reshape(-1)[flat_cell] - seg_vals)
        residual = (
            residual.reshape(3, -1)
            .at[:, flat_cell.reshape(-1)]
            .add(rates.reshape(3, -1))
            .reshape(residual.shape)
        )
        return (residual, rates)

    primal, tangent = jax.jvp(local_terms, (state_pad, seg_pressure), (direc_pad, seg_direction))
    cell_residual, rates = primal
    cell_jvp, rate_tangent = tangent
    rate_total = jnp.sum(rates, axis=0)
    total_tangent = jnp.sum(rate_tangent, axis=0)
    member = (
        group_of[:, 0][:, None] == jnp.arange(group_target.shape[0], dtype=jnp.int32)[None, :]
    ).astype(jnp.float32)
    rates_part = jnp.dot(jnp.sum(rates, axis=2), member, precision=lax.Precision.HIGHEST)
    guide_part = jnp.dot(guide_rate, member, precision=lax.Precision.HIGHEST)
    guide_total = lax.psum(guide_part, "gx")
    group_rates = lax.psum(rates_part, ("gx", "gy"))
    target = (
        jnp.dot(member, group_target, precision=lax.Precision.HIGHEST)
        * guide_rate
        / jnp.dot(member, guide_total, precision=lax.Precision.HIGHEST)
    )
    well_count = seg_pressure.shape[0]
    share = well_count // row_count
    start = row_index * share

    def pick(values):
        return lax.dynamic_slice_in_dim(values, start, share, 0)

    total_sum, tangent_sum = lax.psum((rate_total, total_tangent), "gy")
    equations = segment_terms(parent, seg_head, well_mode, bhp_limit, target)
    seg_full, seg_tan = jax.jvp(equations, (total_sum, seg_pressure), (tangent_sum, seg_direction))
    seg_residual = pick(seg_full)
    seg_jvp = pick(seg_tan)
    return (cell_residual, cell_jvp, seg_residual, seg_jvp, group_rates)


def solution(mesh):
    placed = (
        P(None, "gx", "gy"),
        P(None, None, "gx", "gy"),
        P(None, None, "gx", "gy"),
        P(None, "gx", "gy"),
        P(None, None, "gx", "gy"),
        P(None, None, "gx", "gy"),
        P("gx", None),
        P("gx", None),
        P("gx", None),
        P("gx", None),
        P("gx", None),
        P("gx", None),
        P("gx"),
        P("gx"),
        P("gx"),
        P("gx", None),
        P(),
    )
    return jax.shard_map(
        per_device,
        mesh=mesh,
        in_specs=placed,
        out_specs=(
            P(None, None, "gx", "gy"),
            P(None, None, "gx", "gy"),
            P(("gx", "gy"), None),
            P(("gx", "gy"), None),
            P(),
        ),
        check_vma=False,
    )
```

profile of v0, /device:TPU:1, one launch (start us, length us, event | category | flops | bytes accessed | tf_op | source)
XLA Modules:
  0.0 510.7 jit_solution(14686973665699037031)
XLA Ops:
  2.6 1.0 constant_dynamic-update-slice_fusion
  3.7 1.0 select_dynamic-update-slice_fusion.1
  5.6 1.3 collective-permute-start.1
  6.9 4.6 collective-permute-start
  14.0 1.0 minimum_convert_fusion.2
  15.0 2.0 minimum_convert_fusion
  17.2 32.3 %psum.29 = f32[128]{0:T(128)S(1)} all-reduce(f32[128]{0:T(128)S(1)} %convolution_bitcast_fusion.1), channel_id=1, replica_groups=mesh['gx'=16,'gy'=16] {'gx'}, use_global_device_ids=true, to_apply=%region_5.6 | all-reduce | flops 128 | bytes 1024 | tf_op jit(solution)/shard_map/psum | solution.py:187
  51.9 9.9 %collective-permute-start.3 = (f32[8,2,130,1]{2,0,3,1:T(8,128)S(1)}, f32[8,2,130,1]{2,0,3,1:T(8,128)S(1)}, u32[]{:S(2)}, u32[]{:S(2)}) collective-permute-start(f32[8,2,130,1]{2,0,3,1:T(8,128)S(1)} %copy.106), channel_id=1, source_target_pairs={{1,0},{2,1},{3,2},{4,3},{5,4},{6,5},{7,6},{8,7},{9,8},{10,9},{11,1... | collective-permute-start | bytes 24968 | tf_op jit(solution)/shard_map/ppermute | solution.py:24
  62.4 3.6 collective-permute-start.2
  66.2 43.2 %gather_fusion.5 = f32[4096]{0:T(1024)} fusion(f32[32,128]{1,0:T(8,128)S(1)} %copy-done.1, s32[4096]{0:T(1024)S(1)} %fusion.156), kind=kCustom, calls=%fused_computation.5 | custom fusion | bytes 65536 | tf_op jit(solution)/shard_map/jvp(jit(take_along_axis))/gather | solution.py:71
  109.4 25.6 %gather_fusion.4 = f32[4096]{0:T(1024)S(1)} fusion(f32[32,128]{1,0:T(8,128)S(1)} %copy-done.2, s32[4096]{0:T(1024)S(1)} %fusion.156), kind=kCustom, calls=%fused_computation.4 | custom fusion | bytes 65536 | tf_op jit(solution)/shard_map/jvp(jit(take_along_axis))/gather | solution.py:71
  136.5 1.0 pad_maximum_fusion
  138.1 1.2 fusion.39
  143.0 1.0 pad_maximum_fusion.2
  145.2 8.6 %copy.109 = f32[3,2,128,128]{0,3,2,1:T(8,128)} copy(f32[3,2,128,128]{3,2,1,0:T(8,128)S(1)} %fusion.34) | data formatting | bytes 786432 | tf_op jit(solution)/shard_map/jvp()/sub | solution.py:163
  153.7 8.5 %copy.110 = f32[3,2,128,128]{0,3,2,1:T(8,128)} copy(f32[3,2,128,128]{3,2,1,0:T(8,128)S(1)} %get-tuple-element.106) | data formatting | bytes 786432 | tf_op jit(solution)/shard_map/jvp()/slice | solution.py:133
  162.2 16.5 %gather_fusion = f32[4096,3]{1,0:T(8,128)S(1)} fusion(f32[3,32768]{0,1:T(8,128)} %bitcast.414, s32[4096]{0:T(1024)S(1)} %get-tuple-element.69), kind=kCustom, calls=%fused_computation | custom fusion | bytes 114688 | tf_op jit(solution)/shard_map/jvp()/gather | solution.py:168
  178.8 40.6 %gather_fusion.3 = f32[4096]{0:T(1024)} fusion(f32[32768]{0:T(1024)S(1)} %bitcast.407, s32[4096]{0:T(1024)S(1)} %get-tuple-element.69), kind=kCustom, calls=%fused_computation.3 | custom fusion | bytes 49152 | tf_op jit(solution)/shard_map/jvp()/gather | solution.py:168
  219.4 23.0 %gather_fusion.1 = f32[4096]{0:T(1024)S(1)} fusion(f32[32768]{0:T(1024)S(1)} %bitcast.408, s32[4096]{0:T(1024)S(1)} %get-tuple-element.69), kind=kCustom, calls=%fused_computation.1 | custom fusion | bytes 49152 | tf_op jit(solution)/shard_map/jvp()/gather | solution.py:168
  242.4 36.5 %scatter_custom_fusion = f32[3,32768]{0,1:T(8,128)} fusion(f32[3,32768]{0,1:T(8,128)} %bitcast.409, s32[4096]{0:T(1024)} %bitcast.429, f32[4096,3]{1,0:T(8,128)S(1)} %gather_fusion, f32[4096]{0:T(1024)S(1)} %bitcast.419, f32[4096]{0:T(1024)S(1)} %bitcast.417), kind=kCustom, calls=%fused_computation.15 | custom fusion | flops 36864 | bytes 475136 | tf_op jit(solution)/shard_map/jvp()/scatter-add | solution.py:172
  278.9 10.7 %copy.115 = f32[3,2,128,128]{3,2,1,0:T(8,128)} copy(f32[3,2,128,128]{0,3,2,1:T(8,128)} %bitcast.410) | data formatting | bytes 786432
  289.6 2.5 fusion.31
  292.1 9.5 %copy.111 = f32[3,2,128,128]{0,3,2,1:T(8,128)} copy(f32[3,2,128,128]{3,2,1,0:T(8,128)} %fusion.31) | data formatting | bytes 786432 | tf_op jit(solution)/shard_map/jvp()/sub | solution.py:163
  301.6 8.5 %copy.112 = f32[3,2,128,128]{0,3,2,1:T(8,128)} copy(f32[3,2,128,128]{3,2,1,0:T(8,128)S(1)} %get-tuple-element.105) | data formatting | bytes 786432 | tf_op jit(solution)/shard_map/jvp()/slice | solution.py:133
  310.1 19.9 %gather_fusion.2 = f32[4096,3]{1,0:T(8,128)} fusion(f32[3,32768]{0,1:T(8,128)} %bitcast.415, s32[4096]{0:T(1024)S(1)} %get-tuple-element.69), kind=kCustom, calls=%fused_computation.2 | custom fusion | bytes 114688 | tf_op jit(solution)/shard_map/jvp()/gather | solution.py:168
  330.1 37.0 %scatter_custom_fusion.1 = f32[3,32768]{0,1:T(8,128)} fusion(f32[3,32768]{0,1:T(8,128)} %bitcast.411, s32[4096]{0:T(1024)} %bitcast.430, f32[4096,3]{1,0:T(8,128)} %gather_fusion.2, f32[4096,3]{1,0:T(8,128)S(1)} %gather_fusion, f32[4096]{0:T(1024)S(1)} %bitcast.425, f32[4096]{0:T(1024)S(1)} %bitcast.420, f32[4096]{0:T(1024)S(1)} %bitcast.418), kind=kCustom, calls=%fused_computation.13 | custom fusion | flops 73728 | bytes 2588672 | tf_op jit(solution)/shard_map/jvp()/scatter-add | solution.py:172
  367.1 10.6 %copy.116 = f32[3,2,128,128]{3,2,1,0:T(8,128)} copy(f32[3,2,128,128]{0,3,2,1:T(8,128)} %bitcast.412) | data formatting | bytes 786432
  377.7 4.6 add_reduce_fusion
  382.4 46.0 %all-reduce.4 = (f32[32,128]{1,0:T(8,128)S(1)}, f32[32,128]{1,0:T(8,128)S(1)}) all-reduce(f32[32,128]{1,0:T(8,128)S(1)} %get-tuple-element.55, f32[32,128]{1,0:T(8,128)S(1)} %get-tuple-element.54), channel_id=1, replica_groups=mesh['gx'=16,'gy'=16] {'gy'}, use_global_device_ids=true, to_apply=%region_3.4 | all-reduce | flops 8192 | bytes 65536 | tf_op jit(solution)/shard_map/psum | solution.py:201
  428.4 1.7 fusion.175
  430.2 1.7 fusion.174
  435.5 75.3 %psum.31 = f32[3,128]{1,0:T(4,128)} all-reduce(f32[3,128]{1,0:T(4,128)S(1)} %fusion.157), channel_id=1, replica_groups=mesh['gx'=16,'gy'=16] {'gx','gy'}, use_global_device_ids=true, to_apply=%region_9.10 | all-reduce | flops 384 | bytes 3072 | tf_op jit(solution)/shard_map/psum | solution.py:188
  (105 shorter events, 19.0 us)
Async XLA Ops:
  0.6 431.5 %copy-start = (f32[128]{0:T(128)S(1)}, f32[128]{0:T(128)}, u32[]{:S(2)}) copy-start(f32[128]{0:T(128)} %param.37) | copy-start | bytes 1540
  0.6 10.9 %copy-start.8 = (s32[32,128]{1,0:T(8,128)S(1)}, s32[32,128]{1,0:T(8,128)}, u32[]{:S(2)}) copy-start(s32[32,128]{1,0:T(8,128)} %param.29) | copy-start | bytes 49156
  0.7 11.5 %copy-start.12 = (f32[32,128]{1,0:T(8,128)S(1)}, f32[32,128]{1,0:T(8,128)}, u32[]{:S(2)}) copy-start(f32[32,128]{1,0:T(8,128)} %param.30) | copy-start | bytes 49156
  0.7 11.5 %copy-start.9 = (s32[32,128]{1,0:T(8,128)S(1)}, s32[32,128]{1,0:T(8,128)}, u32[]{:S(2)}) copy-start(s32[32,128]{1,0:T(8,128)} %param.31) | copy-start | bytes 49156
  5.6 45.2 %collective-permute-start.1 = (f32[8,2,1,128]{3,2,1,0:T(1,128)S(1)}, f32[8,2,1,128]{3,2,1,0:T(1,128)S(1)}, u32[]{:S(2)}, u32[]{:S(2)}) collective-permute-start(f32[8,2,1,128]{3,2,1,0:T(1,128)S(1)} %get-tuple-element.89), channel_id=1, source_target_pairs={{16,0},{32,16},{48,32},{64,48},{80,64},{96,80},{112,96},{128,112},... | collective-permute-start | bytes 24584 | tf_op jit(solution)/shard_map/ppermute | solution.py:24
  6.9 43.9 %collective-permute-start = (f32[8,2,1,128]{3,2,1,0:T(1,128)S(1)}, f32[8,2,1,128]{3,2,1,0:T(1,128)S(1)}, u32[]{:S(2)}, u32[]{:S(2)}) collective-permute-start(f32[8,2,1,128]{3,2,1,0:T(1,128)S(1)} %get-tuple-element.88), channel_id=1, source_target_pairs={{0,16},{16,32},{32,48},{48,64},{64,80},{80,96},{96,112},{112,128},... | collective-permute-start | bytes 24584 | tf_op jit(solution)/shard_map/ppermute | solution.py:23
  15.0 2.0 copy-start.16
  15.0 2.0 copy-start.19
  15.0 35.2 %copy-start.2 = (f32[32,128]{1,0:T(8,128)S(1)}, f32[32,128]{1,0:T(8,128)}, u32[]{:S(2)}) copy-start(f32[32,128]{1,0:T(8,128)} %param.27) | copy-start | bytes 49156
  51.3 14.8 %copy-start.1 = (f32[32,128]{1,0:T(8,128)S(1)}, f32[32,128]{1,0:T(8,128)}, u32[]{:S(2)}) copy-start(f32[32,128]{1,0:T(8,128)} %param.28) | copy-start | bytes 49156
  51.9 83.8 %collective-permute-start.3 = (f32[8,2,130,1]{2,0,3,1:T(8,128)S(1)}, f32[8,2,130,1]{2,0,3,1:T(8,128)S(1)}, u32[]{:S(2)}, u32[]{:S(2)}) collective-permute-start(f32[8,2,130,1]{2,0,3,1:T(8,128)S(1)} %copy.106), channel_id=1, source_target_pairs={{1,0},{2,1},{3,2},{4,3},{5,4},{6,5},{7,6},{8,7},{9,8},{10,9},{11,1... | collective-permute-start | bytes 24968 | tf_op jit(solution)/shard_map/ppermute | solution.py:24
  62.4 73.7 %collective-permute-start.2 = (f32[8,2,130,1]{2,0,3,1:T(8,128)S(1)}, f32[8,2,130,1]{2,0,3,1:T(8,128)S(1)}, u32[]{:S(2)}, u32[]{:S(2)}) collective-permute-start(f32[8,2,130,1]{2,0,3,1:T(8,128)S(1)} %copy.105), channel_id=1, source_target_pairs={{0,1},{1,2},{2,3},{3,4},{4,5},{5,6},{6,7},{7,8},{8,9},{9,10},{10,1... | collective-permute-start | bytes 24968 | tf_op jit(solution)/shard_map/ppermute | solution.py:23
  140.7 1.2 copy-start.5
  143.0 1.8 copy-start.6
  143.0 1.8 copy-start.7
  219.4 23.0 %copy-start.11 = (f32[4096]{0:T(1024)S(1)}, f32[4096]{0:T(1024)}, u32[]{:S(2)}) copy-start(f32[4096]{0:T(1024)} %gather_fusion.3) | copy-start | bytes 49156
  278.9 10.7 %copy-start.4 = (f32[3,1,128,128]{3,2,1,0:T(8,128)S(1)}, f32[3,1,128,128]{3,2,1,0:T(8,128)}, u32[]{:S(2)}) copy-start(f32[3,1,128,128]{3,2,1,0:T(8,128)} %get-tuple-element.112) | copy-start | bytes 589828
  377.7 50.7 %copy-start.3 = (bf16[32,128,128]{2,1,0:T(8,128)(2,1)S(1)}, bf16[32,128,128]{2,1,0:T(8,128)(2,1)}, u32[]{:S(2)}) copy-start(bf16[32,128,128]{2,1,0:T(8,128)(2,1)} %minimum_convert_fusion) | copy-start | bytes 3145732
  377.7 52.5 %copy-start.10 = (f32[4096]{0:T(1024)S(1)}, f32[4096]{0:T(1024)}, u32[]{:S(2)}) copy-start(f32[4096]{0:T(1024)} %gather_fusion.5) | copy-start | bytes 49156
  382.3 49.8 %copy-start.14 = (f32[32]{0:T(128)S(1)}, f32[32]{0:T(128)}, u32[]{:S(2)}) copy-start(f32[32]{0:T(128)} %slice_reduce_fusion.2) | copy-start | bytes 388
  382.3 49.8 %copy-start.15 = (s32[32]{0:T(128)S(1)}, s32[32]{0:T(128)}, u32[]{:S(2)}) copy-start(s32[32]{0:T(128)} %param.33) | copy-start | bytes 388
  382.3 49.8 %copy-start.17 = (f32[32]{0:T(128)S(1)}, f32[32]{0:T(128)}, u32[]{:S(2)}) copy-start(f32[32]{0:T(128)} %param.35) | copy-start | bytes 388
  382.3 49.8 %copy-start.18 = (f32[32]{0:T(128)S(1)}, f32[32]{0:T(128)}, u32[]{:S(2)}) copy-start(f32[32]{0:T(128)} %param.34) | copy-start | bytes 388
  382.4 49.8 %copy-start.20 = (s32[32,1]{0,1:T(1,128)S(1)}, s32[32,1]{0,1:T(1,128)}, u32[]{:S(2)}) copy-start(s32[32,1]{0,1:T(1,128)} %param.36) | copy-start | bytes 388
  382.4 49.8 %copy-start.21 = (f32[32]{0:T(128)S(1)}, f32[32]{0:T(128)}, u32[]{:S(2)}) copy-start(f32[32]{0:T(128)} %convolution_bitcast_fusion) | copy-start | bytes 388
  382.4 50.1 %copy-start.13 = (f32[32,128]{1,0:T(8,128)S(1)}, f32[32,128]{1,0:T(8,128)}, u32[]{:S(2)}) copy-start(f32[32,128]{1,0:T(8,128)} %param.32) | copy-start | bytes 49156
where the time goes:
time: 512 us; the launch traced here: 511 us
  local copies, waits for them, and re-layouts  233 us (46%)
  blocking collectives  154 us (30%)
  other arithmetic  93.7 us (18%)
  starting transfers between devices  19.4 us (4%)
  matrix products  9.4 us (2%)
    psum x1, blocking collectives, per_device(): group_rates = lax.psum(rates_part, ('gx', 'gy'))  75.3 us
    scatter-add x2, other arithmetic, local_terms(): residual = residual.reshape(3, -1).at[:, flat_cell.reshape(-1)].add(rates...  73.5 us
    gather x2, local copies, waits for them, and re-layouts, equations(): above = jnp.take_along_axis(seg_vals, parent, axis=1)  68.8 us
    gather x2, local copies, waits for them, and re-layouts, local_terms(): press_in.reshape(-1)[flat_cell] - seg_vals  63.6 us
    psum x1, blocking collectives, per_device(): total_sum, tangent_sum = lax.psum((rate_total, total_tangent), 'gy')  46 us
    gather x2, local copies, waits for them, and re-layouts, local_terms(): mobil_flat[:, flat_cell]  36.5 us
    psum x1, blocking collectives, per_device(): guide_total = lax.psum(guide_part, 'gx')  32.3 us
    unnamed x49, local copies, waits for them, and re-layouts  24.4 us
  transfers between devices with their start and end apart: 4, of which 0 were waited for; matrix products, arithmetic and copies ran while one was open for 15% of the time, Pallas kernels for 0%

commit v1 on v0

v1 whole, which is shorter than its diff:
```python
import jax
import jax.numpy as jnp
from jax import lax
from jax.experimental import pallas as pl
from jax.experimental.pallas import tpu as pltpu
from jax.sharding import PartitionSpec as P

COMPRESS = (0.05, 0.2, 1.0)
VISCOSITY = (0.5, 1.0, 0.2)
DENSITY = (1.0, 0.8, 0.2)
ROCK_COMP = 0.01
GRAVITY = 0.05
UPWIND_WIDTH = 0.02
FRICTION = 0.002
RATE_SCALE = 0.1

MESH = pl.DeviceIdType.MESH
F32 = jnp.float32
BF16 = jnp.bfloat16
NT = (((1,), (1,)), ((), ()))

CH = 32
WELLS_SCATTER = 8


def iota(shape, dim):
    return lax.broadcasted_iota(jnp.int32, shape, dim)


def split2(x):
    high = x.astype(BF16).astype(F32)
    return high, x - high


def split3(x):
    high = x.astype(BF16).astype(F32)
    rest = x - high
    mid = rest.astype(BF16).astype(F32)
    return high, mid, rest - mid


def mobilities(press, water, gas, dpress, dwater, dgas):
    satur = (water, 1.0 - water - gas, gas)
    dsatur = (dwater, -dwater - dgas, dgas)
    volumes, mobil, dmobil = [], [], []
    for a in range(3):
        volume = jnp.exp(COMPRESS[a] * (press - 1.0))
        scaled = satur[a] * volume * (1.0 / VISCOSITY[a])
        volumes.append(volume)
        mobil.append(satur[a] * scaled)
        dmobil.append(scaled * (2.0 * dsatur[a] + COMPRESS[a] * satur[a] * dpress))
    return satur, dsatur, volumes, mobil, dmobil


def upwinding(potential, dpotential):
    half = jnp.tanh(potential * (0.5 / UPWIND_WIDTH))
    upwind = 0.5 + 0.5 * half
    dupwind = (1.0 - half * half) * (0.25 / UPWIND_WIDTH) * dpotential
    return upwind, dupwind


def face(trans, pot, dpot, up, dup, m_in, m_out, dm_in, dm_out):
    jump = m_in - m_out
    mean = m_out + up * jump
    dmean = dm_out + up * (dm_in - dm_out) + dup * jump
    flow = trans * pot
    return flow * mean, flow * dmean + (trans * dpot) * mean


def kernel(
    nx, ny, n_well,
    press, sat, old, pore, trans, direc, seg_p, seg_d, perf, windex, parent, head,
    mode, bhp, guide, group, gtarget,
    res, jvp, seg_res, seg_jvp, grates,
    mhl, gath, rates, mob, colf, edge, halo_tx, halo_rx, msg, rx1, msg2, rx2,
    s_h, r_h, s_1, r_1, s_2, r_2,
):
    cx, cy = press.shape[1], press.shape[2]
    gx, gy = lax.axis_index("gx"), lax.axis_index("gy")
    share = n_well // ny
    state = lambda q, l: (press[l], sat[0, l], sat[1, l], direc[0, l], direc[1, l], direc[2, l])[q]

    barrier = pltpu.get_barrier_semaphore()
    for k in range(1, ny):
        pl.semaphore_signal(barrier, inc=1, device_id={"gy": lax.rem(gy + k, ny)}, device_id_type=MESH)
    for k in range(1, nx):
        pl.semaphore_signal(barrier, inc=1, device_id={"gx": lax.rem(gx + k, nx)}, device_id_type=MESH)

    lane = iota((cx, cy), 1)
    acc = jnp.zeros((cx, cy), F32)
    for l in range(2):
        for q in range(7):
            block = trans.at[0, l] if q == 6 else None
            if q < 6:
                block = (press.at[l], sat.at[0, l], sat.at[1, l], direc.at[0, l], direc.at[1, l], direc.at[2, l])[q]
            row = 2 * q + l
            halo_tx[0, row:row + 1, :] = block[cx - 1:cx, :]
            halo_tx[1, row:row + 1, :] = block[0:1, :]
            lanes = trans[1, l] if q == 6 else block[...]
            acc = jnp.where(lane == row, lanes[:, cy - 1:cy], acc)
            acc = jnp.where(lane == 16 + row, lanes[:, 0:1], acc)
            if q < 6:
                high, low = split2(lanes)
                at = (q * 2 + l) * cx
                mhl[at:at + cx, 0:cy] = high.astype(BF16)
                mhl[at:at + cx, cy:2 * cy] = low.astype(BF16)
    flipped = acc.T
    halo_tx[2] = flipped[0:16]
    halo_tx[3] = flipped[16:32]
    halo_tx[0, 14:16, :] = jnp.zeros((2, cy), F32)
    halo_tx[1, 14:16, :] = jnp.zeros((2, cy), F32)

    pl.semaphore_wait(barrier, nx + ny - 2)

    copies = []

    def send(src, dst, s_sem, r_sem, where):
        copy = pltpu.make_async_remote_copy(
            src_ref=src, dst_ref=dst, send_sem=s_sem, recv_sem=r_sem, device_id=where, device_id_type=MESH
        )
        copy.start()
        return copy

    targets = (
        {"gx": lax.rem(gx + 1, nx)},
        {"gx": lax.rem(gx + nx - 1, nx)},
        {"gy": lax.rem(gy + 1, ny)},
        {"gy": lax.rem(gy + ny - 1, ny)},
    )
    halo = [send(halo_tx.at[f], halo_rx.at[f], s_h.at[f], r_h.at[f], targets[f]) for f in range(4)]

    all_rows = cy * ny
    shift = all_rows.bit_length() - 1
    first_row = gy * cy

    def split_cell(cell):
        return lax.shift_right_logical(cell, shift), (cell & (all_rows - 1)) - first_row

    def gather(c, _):
        w = 2 * c
        cell = jnp.concatenate([perf[pl.ds(w, 1), :], perf[pl.ds(w + 1, 1), :]], axis=1)
        col, row = split_cell(cell)
        hot = (iota((cy, cell.shape[1]), 0) == row).astype(F32).astype(BF16)
        hot = jnp.concatenate([hot, hot], axis=0)
        pick = iota((2 * cx, cell.shape[1]), 0) == col
        for q in range(6):
            got = jnp.dot(mhl[q * 2 * cx:(q + 1) * 2 * cx, :], hot, preferred_element_type=F32)
            got = jnp.sum(jnp.where(pick, got, 0.0), axis=0, keepdims=True)
            half = cell.shape[1] // 2
            gath[q, pl.ds(w, 1), :] = got[:, :half]
            gath[q, pl.ds(w + 1, 1), :] = got[:, half:]
        return 0

    lax.fori_loop(0, n_well // 2, gather, 0)

    col, row = split_cell(perf[...])
    weight = jnp.where((row >= 0) & (row < cy), windex[...], 0.0)
    values = [gath[q] for q in range(6)]
    _, _, _, m, dm = mobilities(*values)
    drop = weight * (values[0] - seg_p[...])
    ddrop = weight * (values[3] - seg_d[...])
    well = iota((n_well, n_well), 0) == iota((n_well, n_well), 1)
    group_col = jnp.sum(jnp.where(well, group[...].astype(F32), 0.0), axis=1, keepdims=True)
    guide_col = jnp.sum(jnp.where(well, guide[...], 0.0), axis=1, keepdims=True)
    groups = gtarget.shape[1]
    member = group_col == iota((n_well, groups), 1).astype(F32)
    guide_part = jnp.sum(jnp.where(member, guide_col, 0.0), axis=0, keepdims=True)
    total = jnp.zeros_like(drop)
    dtotal = jnp.zeros_like(drop)
    parts = []
    for a in range(3):
        rate = m[a] * drop
        drate = dm[a] * drop + m[a] * ddrop
        rates[a] = rate
        rates[3 + a] = drate
        total = total + rate
        dtotal = dtotal + drate
        by_well = jnp.sum(rate, axis=1, keepdims=True)
        parts.append(jnp.sum(jnp.where(member, by_well, 0.0), axis=0, keepdims=True))
    tail = jnp.concatenate(parts + [jnp.zeros_like(parts[0])], axis=0)
    for d in range(ny):
        msg[d, 0:2, :] = total[2 * d:2 * d + 2]
        msg[d, 2:4, :] = dtotal[2 * d:2 * d + 2]
        msg[d, 4:8, :] = tail
    first = []
    for k in range(1, ny):
        to = lax.rem(gy + k, ny)
        first.append(send(msg.at[to], rx1.at[k], s_1.at[k], r_1.at[k], {"gy": to}))

    last = (iota((CH, cy), 1) == cy - 1)
    for l in range(2):
        for q in range(8):
            mob[q, l, cx:cx + 8, :] = jnp.zeros((8, cy), F32)
    colf[:, :, 0:8, :] = jnp.zeros((6, 2, 8, cy), F32)
    for c in range(cx // CH):
        at = slice(c * CH, (c + 1) * CH)
        props = []
        for l in range(2):
            v = (press[l, at], sat[0, l, at], sat[1, l, at], direc[0, l, at], direc[1, l, at], direc[2, l, at])
            satur, dsatur, volume, m, dm = mobilities(*v)
            rock = (1.0 + ROCK_COMP * (v[0] - 1.0)) * pore[l, at]
            drock = ROCK_COMP * v[3] * pore[l, at]
            mob[6, l, at, :] = v[0]
            mob[7, l, at, :] = v[3]
            pot = v[0] - pltpu.roll(v[0], cy - 1, 1)
            dpot = v[3] - pltpu.roll(v[3], cy - 1, 1)
            t = jnp.where(last, 0.0, trans[1, l, at])
            up, dup = upwinding(pot, dpot)
            for a in range(3):
                mob[a, l, at, :] = m[a]
                mob[3 + a, l, at, :] = dm[a]
                mass = satur[a] * volume[a]
                dmass = (dsatur[a] + COMPRESS[a] * satur[a] * v[3]) * volume[a]
                f, df = face(
                    t, pot, dpot, up, dup, m[a], pltpu.roll(m[a], cy - 1, 1), dm[a], pltpu.roll(dm[a], cy - 1, 1)
                )
                res[a, l, at, :] = rock * mass - old[a, l, at] + (f - pltpu.roll(f, 1, 1))
                jvp[a, l, at, :] = drock * mass + rock * dmass + (df - pltpu.roll(df, 1, 1))
            props.append((v[0], v[3], m, dm))
        (p0, d0, m0, dm0), (p1, d1, m1, dm1) = props
        t = trans[2, 0, at]
        for a in range(3):
            pot = p0 - p1 + DENSITY[a] * GRAVITY
            dpot = d0 - d1
            up, dup = upwinding(pot, dpot)
            f, df = face(t, pot, dpot, up, dup, m0[a], m1[a], dm0[a], dm1[a])
            res[a, 0, at, :] += f
            jvp[a, 0, at, :] += df
            res[a, 1, at, :] -= f
            jvp[a, 1, at, :] -= df

    sums = msg[gy]
    for k in range(1, ny):
        first[k - 1].wait_recv()
        sums = sums + rx1[k]
    msg2[0:3, :] = sums[4:7]
    msg2[3:4, :] = guide_part
    msg2[4:8, :] = jnp.zeros((4, groups), F32)
    second = []
    for k in range(1, nx):
        second.append(send(msg2, rx2.at[k], s_2.at[k], r_2.at[k], {"gx": lax.rem(gx + k, nx)}))

    for l in range(2):
        for c in range(cx // CH):
            at = slice(c * CH, (c + 1) * CH)
            nxt = slice(c * CH + 1, (c + 1) * CH + 1)
            here = slice(c * CH + 8, (c + 1) * CH + 8)
            t = trans[0, l, at]
            if c == cx // CH - 1:
                t = jnp.where(iota((CH, cy), 0) == CH - 1, 0.0, t)
            pot = mob[6, l, at] - mob[6, l, nxt]
            dpot = mob[7, l, at] - mob[7, l, nxt]
            up, dup = upwinding(pot, dpot)
            for a in range(3):
                f, df = face(
                    t, pot, dpot, up, dup, mob[a, l, at], mob[a, l, nxt], mob[3 + a, l, at], mob[3 + a, l, nxt]
                )
                colf[a, l, here, :] = f
                colf[3 + a, l, here, :] = df
        for c in range(cx // CH):
            at = slice(c * CH, (c + 1) * CH)
            here = slice(c * CH + 8, (c + 1) * CH + 8)
            prev = slice(c * CH + 7, (c + 1) * CH + 7)
            for a in range(3):
                res[a, l, at, :] += colf[a, l, here] - colf[a, l, prev]
                jvp[a, l, at, :] += colf[3 + a, l, here] - colf[3 + a, l, prev]

    def scatter(c, _):
        hots, sides = [], [[] for _ in range(6)]
        for i in range(WELLS_SCATTER):
            w = c * WELLS_SCATTER + i
            col, row = split_cell(perf[pl.ds(w, 1), :])
            n = col.shape[1]
            hot = (iota((2 * cx, n), 0) == col).astype(F32).astype(BF16)
            hots += [hot, hot]
            hit = (iota((cy, n), 0) == row).astype(F32).astype(BF16).reshape(cy // 16, 16, n)
            for q in range(6):
                for part in split2(rates[q, pl.ds(w, 1), :]):
                    wide = jnp.broadcast_to(part, (16, n)).astype(BF16)
                    sides[q].append((hit * wide[None]).reshape(cy, n))
        hot = jnp.concatenate(hots, axis=1)
        for a in range(3):
            side = jnp.concatenate(
                [jnp.concatenate(sides[a], axis=1), jnp.concatenate(sides[3 + a], axis=1)], axis=0
            )
            out = lax.dot_general(hot, side, NT, preferred_element_type=F32)
            for l in range(2):
                res[a, l] += out[l * cx:(l + 1) * cx, :cy]
                jvp[a, l] += out[l * cx:(l + 1) * cx, cy:]
        return 0

    lax.fori_loop(0, n_well // WELLS_SCATTER, scatter, 0)

    n_seg = perf.shape[1]
    flows, aboves, owns = [], [], []
    for i in range(share):
        w = gy * share + i
        up_of = parent[pl.ds(w, 1), :]
        down = iota((n_seg, n_seg), 0)
        link = down == up_of
        reach = jnp.where(link | (down == iota((n_seg, n_seg), 1)), 1.0, 0.0).astype(BF16)
        for _ in range((n_seg - 1).bit_length()):
            square = jnp.dot(reach, reach, preferred_element_type=F32)
            reach = jnp.minimum(square, 1.0).astype(BF16)
        vals = split3(sums[i:i + 1]) + split3(sums[2 + i:3 + i])
        vals = jnp.concatenate(vals + (jnp.zeros((2, n_seg), F32),), axis=0).astype(BF16)
        flow = lax.dot_general(vals, reach, NT, preferred_element_type=F32)
        own = (seg_p[pl.ds(w, 1), :], seg_d[pl.ds(w, 1), :])
        vals = split3(own[0]) + split3(own[1])
        vals = jnp.concatenate(vals + (jnp.zeros((2, n_seg), F32),), axis=0).astype(BF16)
        above = jnp.dot(vals, jnp.where(link, 1.0, 0.0).astype(BF16), preferred_element_type=F32)
        flows.append((flow[0:1] + flow[1:2] + flow[2:3], flow[3:4] + flow[4:5] + flow[5:6]))
        aboves.append((above[0:1] + above[1:2] + above[2:3], above[3:4] + above[4:5] + above[5:6]))
        owns.append(own)

    for f in range(4):
        halo[f].wait_recv()
    ins, outs = [], []
    for q in range(7):
        r = slice(2 * q, 2 * q + 2)
        ins.append(jnp.concatenate([halo_rx[0, r], halo_tx[0, r], halo_rx[2, r], halo_tx[2, r]], axis=0))
        outs.append(jnp.concatenate([halo_tx[1, r], halo_rx[1, r], halo_tx[3, r], halo_rx[3, r]], axis=0))
    side = iota((8, cy), 0) // 2
    outer = (
        ((side == 0) & (gx == 0)) | ((side == 1) & (gx == nx - 1))
        | ((side == 2) & (gy == 0)) | ((side == 3) & (gy == ny - 1))
    )
    t = jnp.where(outer, 0.0, ins[6])
    pot, dpot = ins[0] - outs[0], ins[3] - outs[3]
    up, dup = upwinding(pot, dpot)
    m_in, m_out = mobilities(*ins[:6]), mobilities(*outs[:6])
    faces = [
        face(t, pot, dpot, up, dup, m_in[3][a], m_out[3][a], m_in[4][a], m_out[4][a]) for a in range(3)
    ]
    edge[...] = jnp.zeros((cx, cy), F32)
    for a in range(3):
        for o, out in enumerate((res, jvp)):
            for l in range(2):
                out[a, l, 0:1, :] -= faces[a][o][l:l + 1]
                out[a, l, cx - 1:cx, :] += faces[a][o][2 + l:3 + l]
            edge[(2 * a + o) * 4:(2 * a + o) * 4 + 4, :] = faces[a][o][4:8]
    turned = edge[...].T
    for a in range(3):
        for o, out in enumerate((res, jvp)):
            for l in range(2):
                at = (2 * a + o) * 4 + l
                delta = jnp.where(lane == 0, -turned[:, at:at + 1], 0.0)
                out[a, l] += jnp.where(lane == cy - 1, turned[:, at + 2:at + 3], delta)

    everything = msg2[...]
    for k in range(1, nx):
        second[k - 1].wait_recv()
        everything = everything + rx2[k]
    grates[...] = everything[0:3]
    guide_total = everything[3:4]

    wells = iota((1, n_well), 1)
    segs = iota((1, n_seg), 1)
    names = iota((1, groups), 1).astype(F32)
    for i in range(share):
        w = gy * share + i
        mine = wells == w
        pick = lambda ref: jnp.sum(jnp.where(mine, ref[...].astype(F32), 0.0), axis=1, keepdims=True)
        chosen = names == pick(group)
        named = lambda row: jnp.sum(jnp.where(chosen, row, 0.0), axis=1, keepdims=True)
        target = named(gtarget[...]) * pick(guide) / named(guide_total)
        rated = pick(mode) == 1.0
        (flow, dflow), (above, dabove), (own, down) = flows[i], aboves[i], owns[i]
        inner = own - above - head[pl.ds(w, 1), :] - FRICTION * flow
        root = jnp.where(rated, RATE_SCALE * (flow - target), own - pick(bhp))
        seg_res[i:i + 1, :] = jnp.where(segs == 0, root, inner)
        inner = down - dabove - FRICTION * dflow
        root = jnp.where(rated, RATE_SCALE * dflow, down)
        seg_jvp[i:i + 1, :] = jnp.where(segs == 0, root, inner)

    for copy in halo + first + second:
        copy.wait_send()


def solution(mesh):
    nx, ny = mesh.shape["gx"], mesh.shape["gy"]

    def per_device(
        pressure, saturations, old_mass, pore_volume, transmissibility, direction, seg_pressure, seg_direction,
        perf_cell, well_index, parent, seg_head, well_mode, bhp_limit, guide_rate, group_of, group_target,
    ):
        n_well, n_seg = perf_cell.shape
        _, cx, cy = pressure.shape
        groups = group_target.shape[0]
        vmem = pl.BlockSpec(memory_space=pltpu.VMEM)
        dma = pltpu.SemaphoreType.DMA
        cells = jax.ShapeDtypeStruct(old_mass.shape, F32)
        segs = jax.ShapeDtypeStruct((n_well // ny, n_seg), F32)
        row = lambda x: x.reshape(1, -1)
        return pl.pallas_call(
            lambda *refs: kernel(nx, ny, n_well, *refs),
            out_shape=(cells, cells, segs, segs, jax.ShapeDtypeStruct((3, groups), F32)),
            in_specs=[vmem] * 17,
            out_specs=(vmem,) * 5,
            scratch_shapes=[
                pltpu.VMEM((12 * cx, 2 * cy), BF16),
                pltpu.VMEM((6, n_well, n_seg), F32),
                pltpu.VMEM((6, n_well, n_seg), F32),
                pltpu.VMEM((8, 2, cx + 8, cy), F32),
                pltpu.VMEM((6, 2, cx + 8, cy), F32),
                pltpu.VMEM((cx, cy), F32),
                pltpu.VMEM((4, 16, cy), F32),
                pltpu.VMEM((4, 16, cy), F32),
                pltpu.VMEM((ny, 8, n_seg), F32),
                pltpu.VMEM((ny, 8, n_seg), F32),
                pltpu.VMEM((8, groups), F32),
                pltpu.VMEM((nx, 8, groups), F32),
                dma((4,)), dma((4,)), dma((ny,)), dma((ny,)), dma((nx,)), dma((nx,)),
            ],
            compiler_params=pltpu.CompilerParams(
                collective_id=0, has_side_effects=True, vmem_limit_bytes=48 * 1024 * 1024
            ),
            name="newton",
        )(
            pressure, saturations, old_mass, pore_volume, transmissibility, direction, seg_pressure, seg_direction,
            perf_cell, well_index, parent, seg_head, row(well_mode), row(bhp_limit), row(guide_rate), row(group_of),
            row(group_target),
        )

    placed = (
        P(None, "gx", "gy"),
        P(None, None, "gx", "gy"),
        P(None, None, "gx", "gy"),
        P(None, "gx", "gy"),
        P(None, None, "gx", "gy"),
        P(None, None, "gx", "gy"),
        P("gx", None),
        P("gx", None),
        P("gx", None),
        P("gx", None),
        P("gx", None),
        P("gx", None),
        P("gx"),
        P("gx"),
        P("gx"),
        P("gx", None),
        P(),
    )
    return jax.shard_map(
        per_device,
        mesh=mesh,
        in_specs=placed,
        out_specs=(
            P(None, None, "gx", "gy"),
            P(None, None, "gx", "gy"),
            P(("gx", "gy"), None),
            P(("gx", "gy"), None),
            P(),
        ),
        check_vma=False,
    )
```

time: 512 us -> 45.6 us (0.09)
  local copies, waits for them, and re-layouts: 233 us -> 13.9 us
  blocking collectives: 154 us -> 0 us
  other arithmetic: 93.7 us -> 0 us
  Pallas kernels: 0 us -> 30.3 us
  starting transfers between devices: 19.4 us -> 0 us
  matrix products: 9.4 us -> 0 us
    gather x6 -> x0, local copies, waits for them, and re-layouts: 169 us -> none  [the longest x2 68.8 us: equations(): above = jnp.take_along_axis(seg_vals, parent, axis=1)]
    psum x3 -> x0, blocking collectives: 154 us -> none  [the longest x1 75.3 us: per_device(): group_rates = lax.psum(rates_part, ('gx', 'gy'))]
    scatter-add x2 -> x0, other arithmetic: 73.5 us -> none  [local_terms(): residual = residual.reshape(3, -1).at[:, flat_cell.reshape(-1)].add(rates...]
    pallas_call x0 -> x1, Pallas kernels: none -> 30.3 us  [per_device(): pl.pallas_call(lambda *refs: kernel(nx, ny, n_well, *refs), out_shape=(ce...]
    slice x11 -> x0, local copies, waits for them, and re-layouts: 19.7 us -> none  [the longest x2 17.1 us: local_terms(): mobil_in = mobility[:, :, 1:-1, 1:-1]]
    ppermute x4 -> x0, starting transfers between devices: 19.4 us -> none  [the longest x2 11.2 us: padded_2(): after = lax.ppermute(first, axis, down)]
    sub x2 -> x0, local copies, waits for them, and re-layouts: 18.1 us -> none  [local_terms(): residual + jnp.pad(flux_layers, ((0, 0), (0, 1), (0, 0), (0, 0)))]
    unnamed x49 -> x39, local copies, waits for them, and re-layouts: 24.4 us -> 13.9 us
  transfers between devices with their start and end apart: 4 -> 0, of which waited for: 0 -> 0; matrix products, arithmetic and copies ran while one was open for 15% -> 0% of each run, Pallas kernels for 0% -> 0%
where the time goes in v1:
time: 45.6 us; the launch traced here: 44.9 us
  Pallas kernels  30.3 us (66%)
  local copies, waits for them, and re-layouts  13.9 us (30%)
  between operations  0.7 us (2%)
    pallas_call x1, Pallas kernels, per_device(): pl.pallas_call(lambda *refs: kernel(nx, ny, n_well, *refs), out_shape=(ce...  30.3 us
    unnamed x39, local copies, waits for them, and re-layouts  13.9 us

profile of v1, /device:TPU:1, one launch (start us, length us, event | category | flops | bytes accessed | tf_op | source)
XLA Modules:
  0.0 44.9 jit_solution(5772121075732744788)
XLA Ops:
  0.6 0.0 copy-start.15
  0.6 0.0 copy-start.16
  0.7 0.0 copy-start.12
  0.7 0.0 copy-start.13
  0.7 0.0 copy-start.14
  0.7 0.6 %copy-done.15 = s32[32,1]{0,1:T(1,128)S(1)} copy-done((s32[32,1]{0,1:T(1,128)S(1)}, s32[32,1]{0,1:T(1,128)}, u32[]{:S(2)}) %copy-start.15) | copy-done | bytes 152
  1.3 0.0 copy-done.16
  1.3 0.0 copy-done.12
  1.3 0.0 copy-done.13
  1.3 0.0 copy-done.14
  1.4 0.0 copy-start
  1.4 1.0 %copy-done = f32[3,2,128,128]{3,2,1,0:T(8,128)S(1)} copy-done((f32[3,2,128,128]{3,2,1,0:T(8,128)S(1)}, f32[3,2,128,128]{3,2,1,0:T(8,128)}, u32[]{:S(2)}) %copy-start) | copy-done | bytes 393240
  2.4 0.0 copy-start.1
  2.4 1.0 %copy-done.1 = f32[3,2,128,128]{3,2,1,0:T(8,128)S(1)} copy-done((f32[3,2,128,128]{3,2,1,0:T(8,128)S(1)}, f32[3,2,128,128]{3,2,1,0:T(8,128)}, u32[]{:S(2)}) %copy-start.1) | copy-done | bytes 393240
  3.4 0.0 copy-start.2
  3.4 1.0 %copy-done.2 = f32[3,2,128,128]{3,2,1,0:T(8,128)S(1)} copy-done((f32[3,2,128,128]{3,2,1,0:T(8,128)S(1)}, f32[3,2,128,128]{3,2,1,0:T(8,128)}, u32[]{:S(2)}) %copy-start.2) | copy-done | bytes 393240
  4.3 0.0 copy-start.3
  4.3 0.9 %copy-done.3 = f32[2,2,128,128]{3,2,1,0:T(8,128)S(1)} copy-done((f32[2,2,128,128]{3,2,1,0:T(8,128)S(1)}, f32[2,2,128,128]{3,2,1,0:T(8,128)}, u32[]{:S(2)}) %copy-start.3) | copy-done | bytes 262168
  5.3 0.9 %copy-done.4 = f32[2,128,128]{2,1,0:T(8,128)S(1)} copy-done((f32[2,128,128]{2,1,0:T(8,128)S(1)}, f32[2,128,128]{2,1,0:T(8,128)}, u32[]{:S(2)}) %copy-start.4) | copy-done | bytes 131096
  6.2 0.9 %copy-done.5 = f32[2,128,128]{2,1,0:T(8,128)S(1)} copy-done((f32[2,128,128]{2,1,0:T(8,128)S(1)}, f32[2,128,128]{2,1,0:T(8,128)}, u32[]{:S(2)}) %copy-start.5) | copy-done | bytes 131096
  7.1 0.7 %copy-done.6 = f32[32,128]{1,0:T(8,128)S(1)} copy-done((f32[32,128]{1,0:T(8,128)S(1)}, f32[32,128]{1,0:T(8,128)}, u32[]{:S(2)}) %copy-start.6) | copy-done | bytes 16408
  7.8 0.7 %copy-done.7 = f32[32,128]{1,0:T(8,128)S(1)} copy-done((f32[32,128]{1,0:T(8,128)S(1)}, f32[32,128]{1,0:T(8,128)}, u32[]{:S(2)}) %copy-start.7) | copy-done | bytes 16408
  8.5 0.7 %copy-done.8 = s32[32,128]{1,0:T(8,128)S(1)} copy-done((s32[32,128]{1,0:T(8,128)S(1)}, s32[32,128]{1,0:T(8,128)}, u32[]{:S(2)}) %copy-start.8) | copy-done | bytes 16408
  9.3 0.7 %copy-done.9 = f32[32,128]{1,0:T(8,128)S(1)} copy-done((f32[32,128]{1,0:T(8,128)S(1)}, f32[32,128]{1,0:T(8,128)}, u32[]{:S(2)}) %copy-start.9) | copy-done | bytes 16408
  10.0 0.7 %copy-done.10 = s32[32,128]{1,0:T(8,128)S(1)} copy-done((s32[32,128]{1,0:T(8,128)S(1)}, s32[32,128]{1,0:T(8,128)}, u32[]{:S(2)}) %copy-start.10) | copy-done | bytes 16408
  10.7 0.7 %copy-done.11 = f32[32,128]{1,0:T(8,128)S(1)} copy-done((f32[32,128]{1,0:T(8,128)S(1)}, f32[32,128]{1,0:T(8,128)}, u32[]{:S(2)}) %copy-start.11) | copy-done | bytes 16408
  11.4 30.3 %newton.1 = (f32[3,2,128,128]{3,2,1,0:T(8,128)S(1)}, f32[3,2,128,128]{3,2,1,0:T(8,128)S(1)}, f32[2,128]{1,0:T(2,128)S(1)}, f32[2,128]{1,0:T(2,128)S(1)}, f32[3,128]{1,0:T(4,128)S(1)}) custom-call(f32[2,128,128]{2,1,0:T(8,128)S(1)} %copy-done.4, f32[2,2,128,128]{3,2,1,0:T(8,128)S(1)} %copy-done.3, f32[3,2,128,128]{3,2,1,0:T(8,128)S(1)} %copy-done, ...), custom_call_target="tpu_custom_call" | custom-call | tf_op jit(solution)/shard_map/newton/pallas_call | solution.py:395
  41.7 0.7 %copy.27 = f32[3,2,128,128]{3,2,1,0:T(8,128)} copy(f32[3,2,128,128]{3,2,1,0:T(8,128)S(1)} %get-tuple-element.10) | data formatting | bytes 786432
  42.4 0.7 %copy.28 = f32[3,2,128,128]{3,2,1,0:T(8,128)} copy(f32[3,2,128,128]{3,2,1,0:T(8,128)S(1)} %get-tuple-element.11) | data formatting | bytes 786432
  43.2 0.6 %copy.29 = f32[2,128]{1,0:T(2,128)} copy(f32[2,128]{1,0:T(2,128)S(1)} %get-tuple-element.12) | data formatting | bytes 2048
  43.7 0.6 %copy.30 = f32[2,128]{1,0:T(2,128)} copy(f32[2,128]{1,0:T(2,128)S(1)} %get-tuple-element.13) | data formatting | bytes 2048
  44.3 0.6 %copy.31 = f32[3,128]{1,0:T(4,128)} copy(f32[3,128]{1,0:T(4,128)S(1)} %get-tuple-element.14) | data formatting | bytes 3072
  (8 shorter events, 0.0 us)
Async XLA Ops:
  0.6 0.7 %copy-start.15 = (s32[32,1]{0,1:T(1,128)S(1)}, s32[32,1]{0,1:T(1,128)}, u32[]{:S(2)}) copy-start(s32[32,1]{0,1:T(1,128)} %param.32) | copy-start | bytes 388
  0.6 0.7 %copy-start.16 = (f32[128]{0:T(128)S(1)}, f32[128]{0:T(128)}, u32[]{:S(2)}) copy-start(f32[128]{0:T(128)} %param.33) | copy-start | bytes 1540
  0.7 0.7 %copy-start.12 = (s32[32]{0:T(128)S(1)}, s32[32]{0:T(128)}, u32[]{:S(2)}) copy-start(s32[32]{0:T(128)} %param.29) | copy-start | bytes 388
  0.7 0.7 %copy-start.13 = (f32[32]{0:T(128)S(1)}, f32[32]{0:T(128)}, u32[]{:S(2)}) copy-start(f32[32]{0:T(128)} %param.30) | copy-start | bytes 388
  0.7 0.7 %copy-start.14 = (f32[32]{0:T(128)S(1)}, f32[32]{0:T(128)}, u32[]{:S(2)}) copy-start(f32[32]{0:T(128)} %param.31) | copy-start | bytes 388
  1.4 1.0 %copy-start = (f32[3,2,128,128]{3,2,1,0:T(8,128)S(1)}, f32[3,2,128,128]{3,2,1,0:T(8,128)}, u32[]{:S(2)}) copy-start(f32[3,2,128,128]{3,2,1,0:T(8,128)} %refs_2_.1) | copy-start | bytes 1179652
  2.4 1.0 %copy-start.1 = (f32[3,2,128,128]{3,2,1,0:T(8,128)S(1)}, f32[3,2,128,128]{3,2,1,0:T(8,128)}, u32[]{:S(2)}) copy-start(f32[3,2,128,128]{3,2,1,0:T(8,128)} %refs_4_.1) | copy-start | bytes 1179652
  3.4 1.0 %copy-start.2 = (f32[3,2,128,128]{3,2,1,0:T(8,128)S(1)}, f32[3,2,128,128]{3,2,1,0:T(8,128)}, u32[]{:S(2)}) copy-start(f32[3,2,128,128]{3,2,1,0:T(8,128)} %refs_5_.1) | copy-start | bytes 1179652
  4.3 0.9 %copy-start.3 = (f32[2,2,128,128]{3,2,1,0:T(8,128)S(1)}, f32[2,2,128,128]{3,2,1,0:T(8,128)}, u32[]{:S(2)}) copy-start(f32[2,2,128,128]{3,2,1,0:T(8,128)} %refs_1_.1) | copy-start | bytes 786436
  5.3 0.9 %copy-start.4 = (f32[2,128,128]{2,1,0:T(8,128)S(1)}, f32[2,128,128]{2,1,0:T(8,128)}, u32[]{:S(2)}) copy-start(f32[2,128,128]{2,1,0:T(8,128)} %refs_0_.1) | copy-start | bytes 393220
  6.2 0.9 %copy-start.5 = (f32[2,128,128]{2,1,0:T(8,128)S(1)}, f32[2,128,128]{2,1,0:T(8,128)}, u32[]{:S(2)}) copy-start(f32[2,128,128]{2,1,0:T(8,128)} %refs_3_.1) | copy-start | bytes 393220
  7.1 0.7 %copy-start.6 = (f32[32,128]{1,0:T(8,128)S(1)}, f32[32,128]{1,0:T(8,128)}, u32[]{:S(2)}) copy-start(f32[32,128]{1,0:T(8,128)} %refs_6_.1) | copy-start | bytes 49156
  7.8 0.7 %copy-start.7 = (f32[32,128]{1,0:T(8,128)S(1)}, f32[32,128]{1,0:T(8,128)}, u32[]{:S(2)}) copy-start(f32[32,128]{1,0:T(8,128)} %refs_7_.1) | copy-start | bytes 49156
  8.5 0.7 %copy-start.8 = (s32[32,128]{1,0:T(8,128)S(1)}, s32[32,128]{1,0:T(8,128)}, u32[]{:S(2)}) copy-start(s32[32,128]{1,0:T(8,128)} %refs_8_.1) | copy-start | bytes 49156
  9.3 0.7 %copy-start.9 = (f32[32,128]{1,0:T(8,128)S(1)}, f32[32,128]{1,0:T(8,128)}, u32[]{:S(2)}) copy-start(f32[32,128]{1,0:T(8,128)} %refs_9_.1) | copy-start | bytes 49156
  10.0 0.7 %copy-start.10 = (s32[32,128]{1,0:T(8,128)S(1)}, s32[32,128]{1,0:T(8,128)}, u32[]{:S(2)}) copy-start(s32[32,128]{1,0:T(8,128)} %refs_10_.1) | copy-start | bytes 49156
  10.7 0.7 %copy-start.11 = (f32[32,128]{1,0:T(8,128)S(1)}, f32[32,128]{1,0:T(8,128)}, u32[]{:S(2)}) copy-start(f32[32,128]{1,0:T(8,128)} %refs_11_.1) | copy-start | bytes 49156

commit v2 on v1

--- a/solution.py
+++ b/solution.py
@@ -20,7 +20,8 @@
 NT = (((1,), (1,)), ((), ()))
 
 CH = 32
-WELLS_SCATTER = 8
+GATHER_UNROLL = 8
+LOAD_ORDER = (0, 1, 5, 8, 9, 6, 7, 15, 14, 16, 4, 2, 3, 10, 11, 12, 13)
 
 
 def iota(shape, dim):
@@ -67,18 +68,33 @@
     return flow * mean, flow * dmean + (trans * dpot) * mean
 
 
-def kernel(
-    nx, ny, n_well,
-    press, sat, old, pore, trans, direc, seg_p, seg_d, perf, windex, parent, head,
-    mode, bhp, guide, group, gtarget,
-    res, jvp, seg_res, seg_jvp, grates,
-    mhl, gath, rates, mob, colf, edge, halo_tx, halo_rx, msg, rx1, msg2, rx2,
-    s_h, r_h, s_1, r_1, s_2, r_2,
-):
+def kernel(nx, ny, *refs):
+    hbm, refs = refs[:17], refs[17:]
+    (res, jvp, seg_res, seg_jvp, grates), refs = refs[:5], refs[5:]
+    held, refs = refs[:17], refs[17:]
+    (
+        mhl, gath, mob, colf, edge, halo_tx, halo_rx, msg, rx1, msg2, rx2,
+        s_in, s_h, r_h, s_1, r_1, s_2, r_2,
+    ) = refs
+    (
+        press, sat, old, pore, trans, direc, seg_p, seg_d, perf, windex, parent, head,
+        mode, bhp, guide, group, gtarget,
+    ) = held
+    loads = [pltpu.make_async_copy(hbm[i], held[i], s_in.at[i]) for i in range(17)]
+    for i in LOAD_ORDER:
+        loads[i].start()
+    waited = set()
+
+    def need(*which):
+        for i in which:
+            if i not in waited:
+                waited.add(i)
+                loads[i].wait()
+
+    n_well = perf.shape[0]
     cx, cy = press.shape[1], press.shape[2]
     gx, gy = lax.axis_index("gx"), lax.axis_index("gy")
     share = n_well // ny
-    state = lambda q, l: (press[l], sat[0, l], sat[1, l], direc[0, l], direc[1, l], direc[2, l])[q]
 
     barrier = pltpu.get_barrier_semaphore()
     for k in range(1, ny):
@@ -86,33 +102,14 @@
     for k in range(1, nx):
         pl.semaphore_signal(barrier, inc=1, device_id={"gx": lax.rem(gx + k, nx)}, device_id_type=MESH)
 
-    lane = iota((cx, cy), 1)
-    acc = jnp.zeros((cx, cy), F32)
+    need(0, 1, 5)
     for l in range(2):
-        for q in range(7):
-            block = trans.at[0, l] if q == 6 else None
-            if q < 6:
-                block = (press.at[l], sat.at[0, l], sat.at[1, l], direc.at[0, l], direc.at[1, l], direc.at[2, l])[q]
-            row = 2 * q + l
-            halo_tx[0, row:row + 1, :] = block[cx - 1:cx, :]
-            halo_tx[1, row:row + 1, :] = block[0:1, :]
-            lanes = trans[1, l] if q == 6 else block[...]
-            acc = jnp.where(lane == row, lanes[:, cy - 1:cy], acc)
-            acc = jnp.where(lane == 16 + row, lanes[:, 0:1], acc)
-            if q < 6:
-                high, low = split2(lanes)
-                at = (q * 2 + l) * cx
-                mhl[at:at + cx, 0:cy] = high.astype(BF16)
-                mhl[at:at + cx, cy:2 * cy] = low.astype(BF16)
-    flipped = acc.T
-    halo_tx[2] = flipped[0:16]
-    halo_tx[3] = flipped[16:32]
-    halo_tx[0, 14:16, :] = jnp.zeros((2, cy), F32)
-    halo_tx[1, 14:16, :] = jnp.zeros((2, cy), F32)
-
-    pl.semaphore_wait(barrier, nx + ny - 2)
-
-    copies = []
+        for q in range(6):
+            block = (press.at[l], sat.at[0, l], sat.at[1, l], direc.at[0, l], direc.at[1, l], direc.at[2, l])[q]
+            high, low = split2(block[...])
+            at = (q * 2 + l) * cx
+            mhl[at:at + cx, 0:cy] = high.astype(BF16)
+            mhl[at:at + cx, cy:2 * cy] = low.astype(BF16)
 
     def send(src, dst, s_sem, r_sem, where):
         copy = pltpu.make_async_remote_copy(
@@ -121,14 +118,7 @@
         copy.start()
         return copy
 
-    targets = (
-        {"gx": lax.rem(gx + 1, nx)},
-        {"gx": lax.rem(gx + nx - 1, nx)},
-        {"gy": lax.rem(gy + 1, ny)},
-        {"gy": lax.rem(gy + ny - 1, ny)},
-    )
-    halo = [send(halo_tx.at[f], halo_rx.at[f], s_h.at[f], r_h.at[f], targets[f]) for f in range(4)]
-
+    need(8)
     all_rows = cy * ny
     shift = all_rows.bit_length() - 1
     first_row = gy * cy
@@ -151,8 +141,9 @@
             gath[q, pl.ds(w + 1, 1), :] = got[:, half:]
         return 0
 
-    lax.fori_loop(0, n_well // 2, gather, 0)
-
+    lax.fori_loop(0, n_well // 2, gather, 0, unroll=GATHER_UNROLL)
+
+    need(9, 6, 7, 15, 14, 16)
     col, row = split_cell(perf[...])
     weight = jnp.where((row >= 0) & (row < cy), windex[...], 0.0)
     values = [gath[q] for q in range(6)]
@@ -171,8 +162,8 @@
     for a in range(3):
         rate = m[a] * drop
         drate = dm[a] * drop + m[a] * ddrop
-        rates[a] = rate
-        rates[3 + a] = drate
+        gath[a] = rate
+        gath[3 + a] = drate
         total = total + rate
         dtotal = dtotal + drate
         by_well = jnp.sum(rate, axis=1, keepdims=True)
@@ -182,11 +173,40 @@
         msg[d, 0:2, :] = total[2 * d:2 * d + 2]
         msg[d, 2:4, :] = dtotal[2 * d:2 * d + 2]
         msg[d, 4:8, :] = tail
+    pl.semaphore_wait(barrier, nx + ny - 2)
     first = []
     for k in range(1, ny):
         to = lax.rem(gy + k, ny)
         first.append(send(msg.at[to], rx1.at[k], s_1.at[k], r_1.at[k], {"gy": to}))
 
+    need(4)
+    lane = iota((cx, cy), 1)
+    acc = jnp.zeros((cx, cy), F32)
+    for l in range(2):
+        for q in range(7):
+            block = (
+                press.at[l], sat.at[0, l], sat.at[1, l], direc.at[0, l], direc.at[1, l], direc.at[2, l], trans.at[0, l]
+            )[q]
+            row = 2 * q + l
+            halo_tx[0, row:row + 1, :] = block[cx - 1:cx, :]
+            halo_tx[1, row:row + 1, :] = block[0:1, :]
+            lanes = trans[1, l] if q == 6 else block[...]
+            acc = jnp.where(lane == row, lanes[:, cy - 1:cy], acc)
+            acc = jnp.where(lane == 16 + row, lanes[:, 0:1], acc)
+    flipped = acc.T
+    halo_tx[2] = flipped[0:16]
+    halo_tx[3] = flipped[16:32]
+    halo_tx[0, 14:16, :] = jnp.zeros((2, cy), F32)
+    halo_tx[1, 14:16, :] = jnp.zeros((2, cy), F32)
+    targets = (
+        {"gx": lax.rem(gx + 1, nx)},
+        {"gx": lax.rem(gx + nx - 1, nx)},
+        {"gy": lax.rem(gy + 1, ny)},
+        {"gy": lax.rem(gy + ny - 1, ny)},
+    )
+    halo = [send(halo_tx.at[f], halo_rx.at[f], s_h.at[f], r_h.at[f], targets[f]) for f in range(4)]
+
+    need(2, 3)
     last = (iota((CH, cy), 1) == cy - 1)
     for l in range(2):
         for q in range(8):
@@ -229,17 +249,6 @@
             res[a, 1, at, :] -= f
             jvp[a, 1, at, :] -= df
 
-    sums = msg[gy]
-    for k in range(1, ny):
-        first[k - 1].wait_recv()
-        sums = sums + rx1[k]
-    msg2[0:3, :] = sums[4:7]
-    msg2[3:4, :] = guide_part
-    msg2[4:8, :] = jnp.zeros((4, groups), F32)
-    second = []
-    for k in range(1, nx):
-        second.append(send(msg2, rx2.at[k], s_2.at[k], r_2.at[k], {"gx": lax.rem(gx + k, nx)}))
-
     for l in range(2):
         for c in range(cx // CH):
             at = slice(c * CH, (c + 1) * CH)
@@ -265,53 +274,63 @@
                 res[a, l, at, :] += colf[a, l, here] - colf[a, l, prev]
                 jvp[a, l, at, :] += colf[3 + a, l, here] - colf[3 + a, l, prev]
 
-    def scatter(c, _):
-        hots, sides = [], [[] for _ in range(6)]
-        for i in range(WELLS_SCATTER):
-            w = c * WELLS_SCATTER + i
-            col, row = split_cell(perf[pl.ds(w, 1), :])
-            n = col.shape[1]
-            hot = (iota((2 * cx, n), 0) == col).astype(F32).astype(BF16)
-            hots += [hot, hot]
-            hit = (iota((cy, n), 0) == row).astype(F32).astype(BF16).reshape(cy // 16, 16, n)
-            for q in range(6):
-                for part in split2(rates[q, pl.ds(w, 1), :]):
-                    wide = jnp.broadcast_to(part, (16, n)).astype(BF16)
-                    sides[q].append((hit * wide[None]).reshape(cy, n))
-        hot = jnp.concatenate(hots, axis=1)
-        for a in range(3):
-            side = jnp.concatenate(
-                [jnp.concatenate(sides[a], axis=1), jnp.concatenate(sides[3 + a], axis=1)], axis=0
-            )
-            out = lax.dot_general(hot, side, NT, preferred_element_type=F32)
-            for l in range(2):
-                res[a, l] += out[l * cx:(l + 1) * cx, :cy]
-                jvp[a, l] += out[l * cx:(l + 1) * cx, cy:]
-        return 0
-
-    lax.fori_loop(0, n_well // WELLS_SCATTER, scatter, 0)
-
+    need(10)
     n_seg = perf.shape[1]
-    flows, aboves, owns = [], [], []
+    links, reaches = [], []
     for i in range(share):
-        w = gy * share + i
-        up_of = parent[pl.ds(w, 1), :]
+        above = parent[pl.ds(gy * share + i, 1), :]
         down = iota((n_seg, n_seg), 0)
-        link = down == up_of
+        link = down == above
         reach = jnp.where(link | (down == iota((n_seg, n_seg), 1)), 1.0, 0.0).astype(BF16)
         for _ in range((n_seg - 1).bit_length()):
             square = jnp.dot(reach, reach, preferred_element_type=F32)
             reach = jnp.minimum(square, 1.0).astype(BF16)
-        vals = split3(sums[i:i + 1]) + split3(sums[2 + i:3 + i])
-        vals = jnp.concatenate(vals + (jnp.zeros((2, n_seg), F32),), axis=0).astype(BF16)
-        flow = lax.dot_general(vals, reach, NT, preferred_element_type=F32)
+        links.append(jnp.where(link, 1.0, 0.0).astype(BF16))
+        reaches.append(reach)
+
+    sums = msg[gy]
+    for k in range(1, ny):
+        first[k - 1].wait_recv()
+        sums = sums + rx1[k]
+    msg2[0:3, :] = sums[4:7]
+    msg2[3:4, :] = guide_part
+    msg2[4:8, :] = jnp.zeros((4, groups), F32)
+    second = []
+    for k in range(1, nx):
+        second.append(send(msg2, rx2.at[k], s_2.at[k], r_2.at[k], {"gx": lax.rem(gx + k, nx)}))
+
+    flows, aboves, owns = [], [], []
+    pad = (jnp.zeros((2, n_seg), F32),)
+    for i in range(share):
+        w = gy * share + i
+        vals = jnp.concatenate(split3(sums[i:i + 1]) + split3(sums[2 + i:3 + i]) + pad, axis=0).astype(BF16)
+        flow = lax.dot_general(vals, reaches[i], NT, preferred_element_type=F32)
         own = (seg_p[pl.ds(w, 1), :], seg_d[pl.ds(w, 1), :])
-        vals = split3(own[0]) + split3(own[1])
-        vals = jnp.concatenate(vals + (jnp.zeros((2, n_seg), F32),), axis=0).astype(BF16)
-        above = jnp.dot(vals, jnp.where(link, 1.0, 0.0).astype(BF16), preferred_element_type=F32)
+        vals = jnp.concatenate(split3(own[0]) + split3(own[1]) + pad, axis=0).astype(BF16)
+        above = jnp.dot(vals, links[i], preferred_element_type=F32)
         flows.append((flow[0:1] + flow[1:2] + flow[2:3], flow[3:4] + flow[4:5] + flow[5:6]))
         aboves.append((above[0:1] + above[1:2] + above[2:3], above[3:4] + above[4:5] + above[5:6]))
         owns.append(own)
+
+    hots, sides = [], [[] for _ in range(6)]
+    for w in range(n_well):
+        col, row = split_cell(perf[w:w + 1, :])
+        hot = (iota((2 * cx, n_seg), 0) == col).astype(F32).astype(BF16)
+        hots += [hot, hot]
+        hit = (iota((cy, n_seg), 0) == row).astype(F32).astype(BF16).reshape(cy // 16, 16, n_seg)
+        for q in range(6):
+            for part in split2(gath[q, w:w + 1, :]):
+                wide = jnp.broadcast_to(part, (16, n_seg)).astype(BF16)
+                sides[q].append((hit * wide[None]).reshape(cy, n_seg))
+    hot = jnp.concatenate(hots, axis=1)
+    for a in range(3):
+        spread = jnp.concatenate(
+            [jnp.concatenate(sides[a], axis=1), jnp.concatenate(sides[3 + a], axis=1)], axis=0
+        )
+        out = lax.dot_general(hot, spread, NT, preferred_element_type=F32)
+        for l in range(2):
+            res[a, l] += out[l * cx:(l + 1) * cx, :cy]
+            jvp[a, l] += out[l * cx:(l + 1) * cx, cy:]
 
     for f in range(4):
         halo[f].wait_recv()
@@ -347,6 +366,7 @@
                 delta = jnp.where(lane == 0, -turned[:, at:at + 1], 0.0)
                 out[a, l] += jnp.where(lane == cy - 1, turned[:, at + 2:at + 3], delta)
 
+    need(11, 12, 13)
     everything = msg2[...]
     for k in range(1, nx):
         second[k - 1].wait_recv()
@@ -377,6 +397,14 @@
         copy.wait_send()
 
 
+def write_out(*refs):
+    copies = [pltpu.make_async_copy(refs[i], refs[5 + i], refs[10].at[i]) for i in range(5)]
+    for copy in copies:
+        copy.start()
+    for copy in copies:
+        copy.wait()
+
+
 def solution(mesh):
     nx, ny = mesh.shape["gx"], mesh.shape["gy"]
 
@@ -388,18 +416,24 @@
         _, cx, cy = pressure.shape
         groups = group_target.shape[0]
         vmem = pl.BlockSpec(memory_space=pltpu.VMEM)
+        hbm = pl.BlockSpec(memory_space=pltpu.HBM)
         dma = pltpu.SemaphoreType.DMA
         cells = jax.ShapeDtypeStruct(old_mass.shape, F32)
         segs = jax.ShapeDtypeStruct((n_well // ny, n_seg), F32)
+        outs = (cells, cells, segs, segs, jax.ShapeDtypeStruct((3, groups), F32))
         row = lambda x: x.reshape(1, -1)
-        return pl.pallas_call(
-            lambda *refs: kernel(nx, ny, n_well, *refs),
-            out_shape=(cells, cells, segs, segs, jax.ShapeDtypeStruct((3, groups), F32)),
-            in_specs=[vmem] * 17,
+        args = (
+            pressure, saturations, old_mass, pore_volume, transmissibility, direction, seg_pressure, seg_direction,
+            perf_cell, well_index, parent, seg_head, row(well_mode), row(bhp_limit), row(guide_rate), row(group_of),
+            row(group_target),
+        )
+        made = pl.pallas_call(
+            lambda *refs: kernel(nx, ny, *refs),
+            out_shape=tuple(pltpu.VMEM(x.shape, x.dtype) for x in outs),
+            in_specs=[hbm] * 17,
             out_specs=(vmem,) * 5,
-            scratch_shapes=[
+            scratch_shapes=[pltpu.VMEM(x.shape, x.dtype) for x in args] + [
                 pltpu.VMEM((12 * cx, 2 * cy), BF16),
-                pltpu.VMEM((6, n_well, n_seg), F32),
                 pltpu.VMEM((6, n_well, n_seg), F32),
                 pltpu.VMEM((8, 2, cx + 8, cy), F32),
                 pltpu.VMEM((6, 2, cx + 8, cy), F32),
@@ -410,17 +444,22 @@
                 pltpu.VMEM((ny, 8, n_seg), F32),
                 pltpu.VMEM((8, groups), F32),
                 pltpu.VMEM((nx, 8, groups), F32),
-                dma((4,)), dma((4,)), dma((ny,)), dma((ny,)), dma((nx,)), dma((nx,)),
+                dma((17,)), dma((4,)), dma((4,)), dma((ny,)), dma((ny,)), dma((nx,)), dma((nx,)),
             ],
             compiler_params=pltpu.CompilerParams(
-                collective_id=0, has_side_effects=True, vmem_limit_bytes=48 * 1024 * 1024
+                collective_id=0, has_side_effects=True, vmem_limit_bytes=60 * 1024 * 1024
             ),
             name="newton",
-        )(
-            pressure, saturations, old_mass, pore_volume, transmissibility, direction, seg_pressure, seg_direction,
-            perf_cell, well_index, parent, seg_head, row(well_mode), row(bhp_limit), row(guide_rate), row(group_of),
-            row(group_target),
-        )
+        )(*[pltpu.with_memory_space_constraint(x, pltpu.HBM) for x in args])
+        return pl.pallas_call(
+            write_out,
+            out_shape=outs,
+            in_specs=[vmem] * 5,
+            out_specs=(hbm,) * 5,
+            scratch_shapes=[dma((5,))],
+            compiler_params=pltpu.CompilerParams(vmem_limit_bytes=1024 * 1024),
+            name="write_out",
+        )(*[pltpu.with_memory_space_constraint(x, pltpu.VMEM) for x in made])
 
     placed = (
         P(None, "gx", "gy"),

time: 45.6 us -> 24.9 us (0.55); the launches traced: 44.9 us -> 24.8 us
  local copies, waits for them, and re-layouts: 13.9 us -> 0 us
  Pallas kernels: 30.3 us -> 24.2 us
    unnamed x39 -> x0, local copies, waits for them, and re-layouts: 13.9 us -> none
    pallas_call x1 -> x2, Pallas kernels: 30.3 us -> 24.2 us  [the longest x1 23.2 us: per_device(): pl.pallas_call(lambda *refs: kernel(nx, ny, *refs), out_shape=tuple((pltp...]
where the time goes in v2:
time: 24.9 us; the launch traced here: 24.8 us
  Pallas kernels  24.2 us (97%)
  between operations  0.65 us (3%)
    pallas_call x1, Pallas kernels, per_device(): pl.pallas_call(lambda *refs: kernel(nx, ny, *refs), out_shape=tuple((pltp...  23.2 us
    pallas_call x1, Pallas kernels, per_device(): pl.pallas_call(write_out, out_shape=outs, in_specs=[vmem] * 5, out_specs=...  0.93 us

profile of v2, /device:TPU:1, one launch (start us, length us, event | category | flops | bytes accessed | tf_op | source)
XLA Modules:
  0.0 24.8 jit_solution(3144443992649534474)
XLA Ops:
  0.6 23.2 %newton.1 = (f32[3,2,128,128]{3,2,1,0:T(8,128)S(1)}, f32[3,2,128,128]{3,2,1,0:T(8,128)S(1)}, f32[2,128]{1,0:T(2,128)S(1)}, f32[2,128]{1,0:T(2,128)S(1)}, f32[3,128]{1,0:T(4,128)S(1)}) custom-call(f32[2,128,128]{2,1,0:T(8,128)} %refs_0_.1, f32[2,2,128,128]{3,2,1,0:T(8,128)} %refs_1_.1, f32[3,2,128,128]{3,2,1,0:T(8,128)} %refs_2_.1, f32[2,128,128]{2,1,0:T(8,128)} %refs_3_.1, ...), custom_call_target="tpu_custom_call" | custom-call | tf_op jit(solution)/shard_map/newton/pallas_call | solution.py:430
  23.9 0.9 %write_out.1 = (f32[3,2,128,128]{3,2,1,0:T(8,128)}, f32[3,2,128,128]{3,2,1,0:T(8,128)}, f32[2,128]{1,0:T(2,128)}, f32[2,128]{1,0:T(2,128)}, f32[3,128]{1,0:T(4,128)}) custom-call(f32[3,2,128,128]{3,2,1,0:T(8,128)S(1)} %get-tuple-element.10.refs_0_, f32[3,2,128,128]{3,2,1,0:T(8,128)S(1)} %get-tuple-element.11.refs_1_, ...), custom_call_target="tpu_custom_call" | custom-call | tf_op jit(solution)/shard_map/write_out/pallas_call | solution.py:454

commit v3 on v2

--- a/solution.py
+++ b/solution.py
@@ -20,7 +20,9 @@
 NT = (((1,), (1,)), ((), ()))
 
 CH = 32
-GATHER_UNROLL = 8
+GATHER_BY_LANE = 10
+GY_ORDER = (8, 7, 9, 6, 10, 5, 11, 4, 12, 3, 13, 2, 14, 1, 15)
+GX_ORDER = (10, 6, 9, 11, 7, 5, 8, 14, 2, 13, 3, 12, 4, 1, 15)
 LOAD_ORDER = (0, 1, 5, 8, 9, 6, 7, 15, 14, 16, 4, 2, 3, 10, 11, 12, 13)
 
 
@@ -68,13 +70,17 @@
     return flow * mean, flow * dmean + (trans * dpot) * mean
 
 
+def partners(order, count):
+    return [k for k in order if k < count] if count <= 16 else list(range(1, count))
+
+
 def kernel(nx, ny, *refs):
     hbm, refs = refs[:17], refs[17:]
     (res, jvp, seg_res, seg_jvp, grates), refs = refs[:5], refs[5:]
     held, refs = refs[:17], refs[17:]
     (
-        mhl, gath, mob, colf, edge, halo_tx, halo_rx, msg, rx1, msg2, rx2,
-        s_in, s_h, r_h, s_1, r_1, s_2, r_2,
+        mhl, gath, mob, colf, edge, halo_tx, halo_rx, msg, rx1, msg2, rx2, part, rxp,
+        s_in, s_h, r_h, s_1, r_1, s_2, r_2, s_p, r_p,
     ) = refs
     (
         press, sat, old, pore, trans, direc, seg_p, seg_d, perf, windex, parent, head,
@@ -102,21 +108,25 @@
     for k in range(1, nx):
         pl.semaphore_signal(barrier, inc=1, device_id={"gx": lax.rem(gx + k, nx)}, device_id_type=MESH)
 
-    need(0, 1, 5)
-    for l in range(2):
-        for q in range(6):
-            block = (press.at[l], sat.at[0, l], sat.at[1, l], direc.at[0, l], direc.at[1, l], direc.at[2, l])[q]
-            high, low = split2(block[...])
+    cells = lambda q, l: (
+        press.at[l], sat.at[0, l], sat.at[1, l], direc.at[0, l], direc.at[1, l], direc.at[2, l]
+    )[q]
+    for q in range(6):
+        need((0, 1, 1, 5, 5, 5)[q])
+        for l in range(2):
+            high, low = split2(cells(q, l)[...])
             at = (q * 2 + l) * cx
             mhl[at:at + cx, 0:cy] = high.astype(BF16)
             mhl[at:at + cx, cy:2 * cy] = low.astype(BF16)
+
+    def wait_all(landed, sem):
+        pltpu.make_async_copy(landed, landed, sem.at[0]).wait()
 
     def send(src, dst, s_sem, r_sem, where):
         copy = pltpu.make_async_remote_copy(
             src_ref=src, dst_ref=dst, send_sem=s_sem, recv_sem=r_sem, device_id=where, device_id_type=MESH
         )
         copy.start()
-        return copy
 
     need(8)
     all_rows = cy * ny
@@ -126,22 +136,44 @@
     def split_cell(cell):
         return lax.shift_right_logical(cell, shift), (cell & (all_rows - 1)) - first_row
 
-    def gather(c, _):
-        w = 2 * c
-        cell = jnp.concatenate([perf[pl.ds(w, 1), :], perf[pl.ds(w + 1, 1), :]], axis=1)
+    def by_product(w):
+        cell = jnp.concatenate([perf[w:w + 1, :], perf[w + 1:w + 2, :]], axis=1)
         col, row = split_cell(cell)
-        hot = (iota((cy, cell.shape[1]), 0) == row).astype(F32).astype(BF16)
+        n = cell.shape[1]
+        hot = (iota((cy, n), 0) == row).astype(F32).astype(BF16)
         hot = jnp.concatenate([hot, hot], axis=0)
-        pick = iota((2 * cx, cell.shape[1]), 0) == col
+        lines = [
+            jnp.dot(mhl[q * 2 * cx:(q + 1) * 2 * cx, :], hot, preferred_element_type=F32) for q in range(6)
+        ]
+        found = [jnp.zeros((8, n), F32)] * 6
+        offset = iota((8, n), 0) - col
+        for i in range(2 * cx // 8):
+            hit = offset == -8 * i
+            found = [jnp.where(hit, lines[q][8 * i:8 * i + 8], found[q]) for q in range(6)]
         for q in range(6):
-            got = jnp.dot(mhl[q * 2 * cx:(q + 1) * 2 * cx, :], hot, preferred_element_type=F32)
-            got = jnp.sum(jnp.where(pick, got, 0.0), axis=0, keepdims=True)
-            half = cell.shape[1] // 2
-            gath[q, pl.ds(w, 1), :] = got[:, :half]
-            gath[q, pl.ds(w + 1, 1), :] = got[:, half:]
-        return 0
-
-    lax.fori_loop(0, n_well // 2, gather, 0, unroll=GATHER_UNROLL)
+            line = jnp.sum(found[q], axis=0, keepdims=True)
+            gath[q, w:w + 1, :] = line[:, :n // 2]
+            gath[q, w + 1:w + 2, :] = line[:, n // 2:]
+
+    def by_lane(w):
+        col, row = split_cell(perf[w:w + 1, :])
+        n = col.shape[1]
+        lanes = jnp.broadcast_to(jnp.clip(row, 0, cy - 1), (8, n))
+        offset = jnp.where((row >= 0) & (row < cy), iota((8, n), 0) - col, 1)
+        found = [jnp.zeros((8, n), F32)] * 6
+        for i in range(2 * cx // 8):
+            l, r = divmod(8 * i, cx)
+            hit = offset == -8 * i
+            for q in range(6):
+                line = jnp.take_along_axis(cells(q, l)[r:r + 8, :], lanes, axis=1, mode="promise_in_bounds")
+                found[q] = jnp.where(hit, line, found[q])
+        for q in range(6):
+            gath[q, w:w + 1, :] = jnp.sum(found[q], axis=0, keepdims=True)
+
+    for w in range(0, n_well - GATHER_BY_LANE, 2):
+        by_product(w)
+    for w in range(n_well - GATHER_BY_LANE, n_well):
+        by_lane(w)
 
     need(9, 6, 7, 15, 14, 16)
     col, row = split_cell(perf[...])
@@ -168,17 +200,18 @@
         dtotal = dtotal + drate
         by_well = jnp.sum(rate, axis=1, keepdims=True)
         parts.append(jnp.sum(jnp.where(member, by_well, 0.0), axis=0, keepdims=True))
-    tail = jnp.concatenate(parts + [jnp.zeros_like(parts[0])], axis=0)
+    for a in range(3):
+        part[a:a + 1, :] = parts[a]
+    pl.semaphore_wait(barrier, nx + ny - 2)
+    for k in partners(GY_ORDER, ny):
+        to = lax.rem(gy + k, ny)
+        send(part.at[pl.ds(0, 3)], rxp.at[k, pl.ds(0, 3)], s_p.at[0], r_p.at[0], {"gy": to})
     for d in range(ny):
         msg[d, 0:2, :] = total[2 * d:2 * d + 2]
         msg[d, 2:4, :] = dtotal[2 * d:2 * d + 2]
-        msg[d, 4:8, :] = tail
-    pl.semaphore_wait(barrier, nx + ny - 2)
-    first = []
-    for k in range(1, ny):
+    for k in partners(GY_ORDER, ny):
         to = lax.rem(gy + k, ny)
-        first.append(send(msg.at[to], rx1.at[k], s_1.at[k], r_1.at[k], {"gy": to}))
-
+        send(msg.at[to, pl.ds(0, 4)], rx1.at[k, pl.ds(0, 4)], s_1.at[0], r_1.at[0], {"gy": to})
     need(4)
     lane = iota((cx, cy), 1)
     acc = jnp.zeros((cx, cy), F32)
@@ -204,7 +237,8 @@
         {"gy": lax.rem(gy + 1, ny)},
         {"gy": lax.rem(gy + ny - 1, ny)},
     )
-    halo = [send(halo_tx.at[f], halo_rx.at[f], s_h.at[f], r_h.at[f], targets[f]) for f in range(4)]
+    for f in range(4):
+        send(halo_tx.at[f], halo_rx.at[f], s_h.at[0], r_h.at[0], targets[f])
 
     need(2, 3)
     last = (iota((CH, cy), 1) == cy - 1)
@@ -288,29 +322,15 @@
         links.append(jnp.where(link, 1.0, 0.0).astype(BF16))
         reaches.append(reach)
 
-    sums = msg[gy]
+    sums = part[0:3, :]
+    wait_all(rxp.at[pl.ds(1, ny - 1), pl.ds(0, 3)], r_p)
     for k in range(1, ny):
-        first[k - 1].wait_recv()
-        sums = sums + rx1[k]
-    msg2[0:3, :] = sums[4:7]
+        sums = sums + rxp[k, 0:3, :]
+    msg2[0:3, :] = sums
     msg2[3:4, :] = guide_part
-    msg2[4:8, :] = jnp.zeros((4, groups), F32)
-    second = []
-    for k in range(1, nx):
-        second.append(send(msg2, rx2.at[k], s_2.at[k], r_2.at[k], {"gx": lax.rem(gx + k, nx)}))
-
-    flows, aboves, owns = [], [], []
-    pad = (jnp.zeros((2, n_seg), F32),)
-    for i in range(share):
-        w = gy * share + i
-        vals = jnp.concatenate(split3(sums[i:i + 1]) + split3(sums[2 + i:3 + i]) + pad, axis=0).astype(BF16)
-        flow = lax.dot_general(vals, reaches[i], NT, preferred_element_type=F32)
-        own = (seg_p[pl.ds(w, 1), :], seg_d[pl.ds(w, 1), :])
-        vals = jnp.concatenate(split3(own[0]) + split3(own[1]) + pad, axis=0).astype(BF16)
-        above = jnp.dot(vals, links[i], preferred_element_type=F32)
-        flows.append((flow[0:1] + flow[1:2] + flow[2:3], flow[3:4] + flow[4:5] + flow[5:6]))
-        aboves.append((above[0:1] + above[1:2] + above[2:3], above[3:4] + above[4:5] + above[5:6]))
-        owns.append(own)
+    for k in partners(GX_ORDER, nx):
+        to = lax.rem(gx + k, nx)
+        send(msg2.at[pl.ds(0, 4)], rx2.at[k, pl.ds(0, 4)], s_2.at[0], r_2.at[0], {"gx": to})
 
     hots, sides = [], [[] for _ in range(6)]
     for w in range(n_well):
@@ -332,8 +352,7 @@
             res[a, l] += out[l * cx:(l + 1) * cx, :cy]
             jvp[a, l] += out[l * cx:(l + 1) * cx, cy:]
 
-    for f in range(4):
-        halo[f].wait_recv()
+    wait_all(halo_rx, r_h)
     ins, outs = [], []
     for q in range(7):
         r = slice(2 * q, 2 * q + 2)
@@ -366,11 +385,29 @@
                 delta = jnp.where(lane == 0, -turned[:, at:at + 1], 0.0)
                 out[a, l] += jnp.where(lane == cy - 1, turned[:, at + 2:at + 3], delta)
 
+    sums = msg[gy, 0:4, :]
+    wait_all(rx1.at[pl.ds(1, ny - 1), pl.ds(0, 4)], r_1)
+    for k in range(1, ny):
+        sums = sums + rx1[k, 0:4, :]
+
+    flows, aboves, owns = [], [], []
+    pad = (jnp.zeros((2, n_seg), F32),)
+    for i in range(share):
+        w = gy * share + i
+        vals = jnp.concatenate(split3(sums[i:i + 1]) + split3(sums[2 + i:3 + i]) + pad, axis=0).astype(BF16)
+        flow = lax.dot_general(vals, reaches[i], NT, preferred_element_type=F32)
+        own = (seg_p[pl.ds(w, 1), :], seg_d[pl.ds(w, 1), :])
+        vals = jnp.concatenate(split3(own[0]) + split3(own[1]) + pad, axis=0).astype(BF16)
+        above = jnp.dot(vals, links[i], preferred_element_type=F32)
+        flows.append((flow[0:1] + flow[1:2] + flow[2:3], flow[3:4] + flow[4:5] + flow[5:6]))
+        aboves.append((above[0:1] + above[1:2] + above[2:3], above[3:4] + above[4:5] + above[5:6]))
+        owns.append(own)
+
     need(11, 12, 13)
-    everything = msg2[...]
+    everything = msg2[0:4, :]
+    wait_all(rx2.at[pl.ds(1, nx - 1), pl.ds(0, 4)], r_2)
     for k in range(1, nx):
-        second[k - 1].wait_recv()
-        everything = everything + rx2[k]
+        everything = everything + rx2[k, 0:4, :]
     grates[...] = everything[0:3]
     guide_total = everything[3:4]
 
@@ -393,8 +430,10 @@
         root = jnp.where(rated, RATE_SCALE * dflow, down)
         seg_jvp[i:i + 1, :] = jnp.where(segs == 0, root, inner)
 
-    for copy in halo + first + second:
-        copy.wait_send()
+    wait_all(halo_rx, s_h)
+    wait_all(rxp.at[pl.ds(1, ny - 1), pl.ds(0, 3)], s_p)
+    wait_all(rx1.at[pl.ds(1, ny - 1), pl.ds(0, 4)], s_1)
+    wait_all(rx2.at[pl.ds(1, nx - 1), pl.ds(0, 4)], s_2)
 
 
 def write_out(*refs):
@@ -444,7 +483,9 @@
                 pltpu.VMEM((ny, 8, n_seg), F32),
                 pltpu.VMEM((8, groups), F32),
                 pltpu.VMEM((nx, 8, groups), F32),
-                dma((17,)), dma((4,)), dma((4,)), dma((ny,)), dma((ny,)), dma((nx,)), dma((nx,)),
+                pltpu.VMEM((8, groups), F32),
+                pltpu.VMEM((ny, 8, groups), F32),
+                dma((17,)), dma((1,)), dma((1,)), dma((1,)), dma((1,)), dma((1,)), dma((1,)), dma((1,)), dma((1,)),
             ],
             compiler_params=pltpu.CompilerParams(
                 collective_id=0, has_side_effects=True, vmem_limit_bytes=60 * 1024 * 1024

time: 24.9 us -> 23.5 us (0.944)
  Pallas kernels: 24.2 us -> 22.8 us
    pallas_call x1, Pallas kernels: 23.2 us -> 21.8 us  [per_device(): pl.pallas_call(lambda *refs: kernel(nx, ny, *refs), out_shape=tuple((pltp...]
where the time goes in v3:
time: 23.5 us; the launch traced here: 23.4 us
  Pallas kernels  22.8 us (97%)
  between operations  0.65 us (3%)
    pallas_call x1, Pallas kernels, per_device(): pl.pallas_call(lambda *refs: kernel(nx, ny, *refs), out_shape=tuple((pltp...  21.8 us
    pallas_call x1, Pallas kernels, per_device(): pl.pallas_call(write_out, out_shape=outs, in_specs=[vmem] * 5, out_specs=...  0.93 us

profile of v3, /device:TPU:1, one launch (start us, length us, event | category | flops | bytes accessed | tf_op | source)
XLA Modules:
  0.0 23.4 jit_solution(2440190800868118217)
XLA Ops:
  0.6 21.8 %newton.1 = (f32[3,2,128,128]{3,2,1,0:T(8,128)S(1)}, f32[3,2,128,128]{3,2,1,0:T(8,128)S(1)}, f32[2,128]{1,0:T(2,128)S(1)}, f32[2,128]{1,0:T(2,128)S(1)}, f32[3,128]{1,0:T(4,128)S(1)}) custom-call(f32[2,128,128]{2,1,0:T(8,128)} %refs_0_.1, f32[2,2,128,128]{3,2,1,0:T(8,128)} %refs_1_.1, f32[3,2,128,128]{3,2,1,0:T(8,128)} %refs_2_.1, f32[2,128,128]{2,1,0:T(8,128)} %refs_3_.1, ...), custom_call_target="tpu_custom_call" | custom-call | tf_op jit(solution)/shard_map/newton/pallas_call | solution.py:469
  22.5 0.9 %write_out.1 = (f32[3,2,128,128]{3,2,1,0:T(8,128)}, f32[3,2,128,128]{3,2,1,0:T(8,128)}, f32[2,128]{1,0:T(2,128)}, f32[2,128]{1,0:T(2,128)}, f32[3,128]{1,0:T(4,128)}) custom-call(f32[3,2,128,128]{3,2,1,0:T(8,128)S(1)} %get-tuple-element.10.refs_0_, f32[3,2,128,128]{3,2,1,0:T(8,128)S(1)} %get-tuple-element.11.refs_1_, ...), custom_call_target="tpu_custom_call" | custom-call | tf_op jit(solution)/shard_map/write_out/pallas_call | solution.py:495

commit v4 on v3

--- a/solution.py
+++ b/solution.py
@@ -20,10 +20,12 @@
 NT = (((1,), (1,)), ((), ()))
 
 CH = 32
+EXCHANGE_AT = 0.45
+SPREAD_WELLS = 8
 GATHER_BY_LANE = 10
 GY_ORDER = (8, 7, 9, 6, 10, 5, 11, 4, 12, 3, 13, 2, 14, 1, 15)
 GX_ORDER = (10, 6, 9, 11, 7, 5, 8, 14, 2, 13, 3, 12, 4, 1, 15)
-LOAD_ORDER = (0, 1, 5, 8, 9, 6, 7, 15, 14, 16, 4, 2, 3, 10, 11, 12, 13)
+LOAD_ORDER = (8, 0, 1, 9, 6, 15, 5, 7, 14, 16, 4, 2, 3, 10, 11, 12, 13)
 
 
 def iota(shape, dim):
@@ -70,6 +72,146 @@
     return flow * mean, flow * dmean + (trans * dpot) * mean
 
 
+def weave(exchange, *strands):
+    counts = [n for n, _ in strands]
+    places = sorted((((i + 0.5) / n, j) for j, n in enumerate(counts) for i in range(n)))
+    for i, (_, j) in enumerate(places):
+        if i == round(EXCHANGE_AT * len(places)):
+            exchange()
+        next(strands[j][1])
+    if EXCHANGE_AT == 1:
+        exchange()
+
+
+def spread_rates(perf, gath, split_cell, scat, cx, cy):
+    n_well, n_seg = perf.shape
+
+    def pieces():
+        for start in range(0, n_well, SPREAD_WELLS):
+            hots, hits = [], []
+            for w in range(start, start + SPREAD_WELLS):
+                col, row = split_cell(perf[w:w + 1, :])
+                hot = (iota((2 * cx, n_seg), 0) == col).astype(F32).astype(BF16)
+                hots += [hot, hot]
+                hit = (iota((cy, n_seg), 0) == row).astype(F32).astype(BF16)
+                hits.append(hit.reshape(cy // 16, 16, n_seg))
+            hot = jnp.concatenate(hots, axis=1)
+            for a in range(3):
+                sides = []
+                for q in (a, 3 + a):
+                    side = []
+                    for i in range(SPREAD_WELLS):
+                        for part in split2(gath[q, start + i:start + i + 1, :]):
+                            wide = jnp.broadcast_to(part, (16, n_seg)).astype(BF16)
+                            side.append((hits[i] * wide[None]).reshape(cy, n_seg))
+                    sides.append(jnp.concatenate(side, axis=1))
+                out = lax.dot_general(hot, jnp.concatenate(sides, axis=0), NT, preferred_element_type=F32)
+                if start == 0:
+                    scat[a] = out
+                else:
+                    scat[a] += out
+                yield
+
+    return 3 * (n_well // SPREAD_WELLS), pieces()
+
+
+def descent(parent, first, share, links, reaches):
+    n_seg = parent.shape[1]
+    levels = (n_seg - 1).bit_length()
+
+    def pieces():
+        down = iota((n_seg, n_seg), 0)
+        for i in range(share):
+            link = down == parent[pl.ds(first + i, 1), :]
+            links.append(jnp.where(link, 1.0, 0.0).astype(BF16))
+            reach = jnp.where(link | (down == iota((n_seg, n_seg), 1)), 1.0, 0.0).astype(BF16)
+            reaches.append(reach)
+        for _ in range(levels):
+            squares = [jnp.dot(reach, reach, preferred_element_type=F32) for reach in reaches]
+            reaches[:] = [jnp.minimum(square, 1.0).astype(BF16) for square in squares]
+            yield
+
+    return levels, pieces()
+
+
+def cell_terms(press, sat, old, pore, trans, direc, res, jvp, mob, colf):
+    cx, cy = press.shape[1], press.shape[2]
+    steps = cx // CH
+
+    def pieces():
+        last = (iota((CH, cy), 1) == cy - 1)
+        for l in range(2):
+            for q in range(8):
+                mob[q, l, cx:cx + 8, :] = jnp.zeros((8, cy), F32)
+        colf[:, :, 0:8, :] = jnp.zeros((6, 2, 8, cy), F32)
+        for c in range(cx // CH):
+            at = slice(c * CH, (c + 1) * CH)
+            props = []
+            for l in range(2):
+                v = (press[l, at], sat[0, l, at], sat[1, l, at], direc[0, l, at], direc[1, l, at], direc[2, l, at])
+                satur, dsatur, volume, m, dm = mobilities(*v)
+                rock = (1.0 + ROCK_COMP * (v[0] - 1.0)) * pore[l, at]
+                drock = ROCK_COMP * v[3] * pore[l, at]
+                mob[6, l, at, :] = v[0]
+                mob[7, l, at, :] = v[3]
+                pot = v[0] - pltpu.roll(v[0], cy - 1, 1)
+                dpot = v[3] - pltpu.roll(v[3], cy - 1, 1)
+                t = jnp.where(last, 0.0, trans[1, l, at])
+                up, dup = upwinding(pot, dpot)
+                for a in range(3):
+                    mob[a, l, at, :] = m[a]
+                    mob[3 + a, l, at, :] = dm[a]
+                    mass = satur[a] * volume[a]
+                    dmass = (dsatur[a] + COMPRESS[a] * satur[a] * v[3]) * volume[a]
+                    f, df = face(
+                        t, pot, dpot, up, dup, m[a], pltpu.roll(m[a], cy - 1, 1), dm[a], pltpu.roll(dm[a], cy - 1, 1)
+                    )
+                    res[a, l, at, :] = rock * mass - old[a, l, at] + (f - pltpu.roll(f, 1, 1))
+                    jvp[a, l, at, :] = drock * mass + rock * dmass + (df - pltpu.roll(df, 1, 1))
+                props.append((v[0], v[3], m, dm))
+            (p0, d0, m0, dm0), (p1, d1, m1, dm1) = props
+            t = trans[2, 0, at]
+            for a in range(3):
+                pot = p0 - p1 + DENSITY[a] * GRAVITY
+                dpot = d0 - d1
+                up, dup = upwinding(pot, dpot)
+                f, df = face(t, pot, dpot, up, dup, m0[a], m1[a], dm0[a], dm1[a])
+                res[a, 0, at, :] += f
+                jvp[a, 0, at, :] += df
+                res[a, 1, at, :] -= f
+                jvp[a, 1, at, :] -= df
+            yield
+
+        for l in range(2):
+            for c in range(cx // CH):
+                at = slice(c * CH, (c + 1) * CH)
+                nxt = slice(c * CH + 1, (c + 1) * CH + 1)
+                here = slice(c * CH + 8, (c + 1) * CH + 8)
+                t = trans[0, l, at]
+                if c == cx // CH - 1:
+                    t = jnp.where(iota((CH, cy), 0) == CH - 1, 0.0, t)
+                pot = mob[6, l, at] - mob[6, l, nxt]
+                dpot = mob[7, l, at] - mob[7, l, nxt]
+                up, dup = upwinding(pot, dpot)
+                for a in range(3):
+                    f, df = face(
+                        t, pot, dpot, up, dup, mob[a, l, at], mob[a, l, nxt], mob[3 + a, l, at], mob[3 + a, l, nxt]
+                    )
+                    colf[a, l, here, :] = f
+                    colf[3 + a, l, here, :] = df
+                yield
+            for c in range(cx // CH):
+                at = slice(c * CH, (c + 1) * CH)
+                here = slice(c * CH + 8, (c + 1) * CH + 8)
+                prev = slice(c * CH + 7, (c + 1) * CH + 7)
+                for a in range(3):
+                    res[a, l, at, :] += colf[a, l, here] - colf[a, l, prev]
+                    jvp[a, l, at, :] += colf[3 + a, l, here] - colf[3 + a, l, prev]
+                yield
+
+    return 5 * steps, pieces()
+
+
 def partners(order, count):
     return [k for k in order if k < count] if count <= 16 else list(range(1, count))
 
@@ -79,8 +221,8 @@
     (res, jvp, seg_res, seg_jvp, grates), refs = refs[:5], refs[5:]
     held, refs = refs[:17], refs[17:]
     (
-        mhl, gath, mob, colf, edge, halo_tx, halo_rx, msg, rx1, msg2, rx2, part, rxp,
-        s_in, s_h, r_h, s_1, r_1, s_2, r_2, s_p, r_p,
+        mhl, gath, mob, colf, edge, halo_tx, halo_rx, msg, rx1, msg2, rx2, part, rxp, scat, aims, rxg,
+        s_in, s_h, r_h, s_1, r_1, s_2, r_2, s_p, r_p, s_g, r_g,
     ) = refs
     (
         press, sat, old, pore, trans, direc, seg_p, seg_d, perf, windex, parent, head,
@@ -111,13 +253,14 @@
     cells = lambda q, l: (
         press.at[l], sat.at[0, l], sat.at[1, l], direc.at[0, l], direc.at[1, l], direc.at[2, l]
     )[q]
-    for q in range(6):
-        need((0, 1, 1, 5, 5, 5)[q])
-        for l in range(2):
-            high, low = split2(cells(q, l)[...])
-            at = (q * 2 + l) * cx
-            mhl[at:at + cx, 0:cy] = high.astype(BF16)
-            mhl[at:at + cx, cy:2 * cy] = low.astype(BF16)
+    def split_cells(qs):
+        for q in qs:
+            need((0, 1, 1, 5, 5, 5)[q])
+            for l in range(2):
+                high, low = split2(cells(q, l)[...])
+                at = (q * 2 + l) * cx
+                mhl[at:at + cx, 0:cy] = high.astype(BF16)
+                mhl[at:at + cx, cy:2 * cy] = low.astype(BF16)
 
     def wait_all(landed, sem):
         pltpu.make_async_copy(landed, landed, sem.at[0]).wait()
@@ -128,7 +271,8 @@
         )
         copy.start()
 
-    need(8)
+    need(8, 9, 6, 15)
+    split_cells(range(3))
     all_rows = cy * ny
     shift = all_rows.bit_length() - 1
     first_row = gy * cy
@@ -136,76 +280,83 @@
     def split_cell(cell):
         return lax.shift_right_logical(cell, shift), (cell & (all_rows - 1)) - first_row
 
-    def by_product(w):
+    def by_product(w, qs):
         cell = jnp.concatenate([perf[w:w + 1, :], perf[w + 1:w + 2, :]], axis=1)
         col, row = split_cell(cell)
         n = cell.shape[1]
         hot = (iota((cy, n), 0) == row).astype(F32).astype(BF16)
         hot = jnp.concatenate([hot, hot], axis=0)
-        lines = [
-            jnp.dot(mhl[q * 2 * cx:(q + 1) * 2 * cx, :], hot, preferred_element_type=F32) for q in range(6)
-        ]
-        found = [jnp.zeros((8, n), F32)] * 6
+        lines = [jnp.dot(mhl[q * 2 * cx:(q + 1) * 2 * cx, :], hot, preferred_element_type=F32) for q in qs]
+        found = [jnp.zeros((8, n), F32)] * len(qs)
         offset = iota((8, n), 0) - col
         for i in range(2 * cx // 8):
             hit = offset == -8 * i
-            found = [jnp.where(hit, lines[q][8 * i:8 * i + 8], found[q]) for q in range(6)]
-        for q in range(6):
-            line = jnp.sum(found[q], axis=0, keepdims=True)
+            found = [jnp.where(hit, line[8 * i:8 * i + 8], got) for line, got in zip(lines, found)]
+        for q, got in zip(qs, found):
+            line = jnp.sum(got, axis=0, keepdims=True)
             gath[q, w:w + 1, :] = line[:, :n // 2]
             gath[q, w + 1:w + 2, :] = line[:, n // 2:]
 
-    def by_lane(w):
+    def by_lane(w, qs):
         col, row = split_cell(perf[w:w + 1, :])
         n = col.shape[1]
         lanes = jnp.broadcast_to(jnp.clip(row, 0, cy - 1), (8, n))
         offset = jnp.where((row >= 0) & (row < cy), iota((8, n), 0) - col, 1)
-        found = [jnp.zeros((8, n), F32)] * 6
+        found = [jnp.zeros((8, n), F32)] * len(qs)
         for i in range(2 * cx // 8):
             l, r = divmod(8 * i, cx)
             hit = offset == -8 * i
-            for q in range(6):
+            for j, q in enumerate(qs):
                 line = jnp.take_along_axis(cells(q, l)[r:r + 8, :], lanes, axis=1, mode="promise_in_bounds")
-                found[q] = jnp.where(hit, line, found[q])
-        for q in range(6):
-            gath[q, w:w + 1, :] = jnp.sum(found[q], axis=0, keepdims=True)
-
-    for w in range(0, n_well - GATHER_BY_LANE, 2):
-        by_product(w)
-    for w in range(n_well - GATHER_BY_LANE, n_well):
-        by_lane(w)
-
-    need(9, 6, 7, 15, 14, 16)
+                found[j] = jnp.where(hit, line, found[j])
+        for q, got in zip(qs, found):
+            gath[q, w:w + 1, :] = jnp.sum(got, axis=0, keepdims=True)
+
+    def gather(qs):
+        for w in range(0, n_well - GATHER_BY_LANE, 2):
+            by_product(w, qs)
+        for w in range(n_well - GATHER_BY_LANE, n_well):
+            by_lane(w, qs)
+
+    gather(range(3))
     col, row = split_cell(perf[...])
     weight = jnp.where((row >= 0) & (row < cy), windex[...], 0.0)
-    values = [gath[q] for q in range(6)]
-    _, _, _, m, dm = mobilities(*values)
+    values = [gath[q] for q in range(3)]
+    _, _, _, m, _ = mobilities(*values, *values)
     drop = weight * (values[0] - seg_p[...])
-    ddrop = weight * (values[3] - seg_d[...])
     well = iota((n_well, n_well), 0) == iota((n_well, n_well), 1)
     group_col = jnp.sum(jnp.where(well, group[...].astype(F32), 0.0), axis=1, keepdims=True)
-    guide_col = jnp.sum(jnp.where(well, guide[...], 0.0), axis=1, keepdims=True)
     groups = gtarget.shape[1]
     member = group_col == iota((n_well, groups), 1).astype(F32)
-    guide_part = jnp.sum(jnp.where(member, guide_col, 0.0), axis=0, keepdims=True)
-    total = jnp.zeros_like(drop)
-    dtotal = jnp.zeros_like(drop)
-    parts = []
+    rates = [m[a] * drop for a in range(3)]
     for a in range(3):
-        rate = m[a] * drop
-        drate = dm[a] * drop + m[a] * ddrop
-        gath[a] = rate
-        gath[3 + a] = drate
-        total = total + rate
-        dtotal = dtotal + drate
-        by_well = jnp.sum(rate, axis=1, keepdims=True)
-        parts.append(jnp.sum(jnp.where(member, by_well, 0.0), axis=0, keepdims=True))
-    for a in range(3):
-        part[a:a + 1, :] = parts[a]
+        by_well = jnp.sum(rates[a], axis=1, keepdims=True)
+        part[a:a + 1, :] = jnp.sum(jnp.where(member, by_well, 0.0), axis=0, keepdims=True)
     pl.semaphore_wait(barrier, nx + ny - 2)
     for k in partners(GY_ORDER, ny):
         to = lax.rem(gy + k, ny)
         send(part.at[pl.ds(0, 3)], rxp.at[k, pl.ds(0, 3)], s_p.at[0], r_p.at[0], {"gy": to})
+
+    need(14, 16, 7)
+    guide_col = jnp.sum(jnp.where(well, guide[...], 0.0), axis=1, keepdims=True)
+    guide_part = jnp.sum(jnp.where(member, guide_col, 0.0), axis=0, keepdims=True)
+    aims[...] = guide_part
+    for k in partners(GX_ORDER, nx):
+        to = lax.rem(gx + k, nx)
+        send(aims, rxg.at[k], s_g.at[0], r_g.at[0], {"gx": to})
+
+    split_cells(range(3, 6))
+    gather(range(3, 6))
+    slopes = [gath[q] for q in range(3, 6)]
+    _, _, _, m, dm = mobilities(*values, *slopes)
+    ddrop = weight * (slopes[0] - seg_d[...])
+    total = rates[0] + rates[1] + rates[2]
+    dtotal = jnp.zeros_like(drop)
+    for a in range(3):
+        drate = dm[a] * drop + m[a] * ddrop
+        gath[a] = rates[a]
+        gath[3 + a] = drate
+        dtotal = dtotal + drate
     for d in range(ny):
         msg[d, 0:2, :] = total[2 * d:2 * d + 2]
         msg[d, 2:4, :] = dtotal[2 * d:2 * d + 2]
@@ -240,117 +391,25 @@
     for f in range(4):
         send(halo_tx.at[f], halo_rx.at[f], s_h.at[0], r_h.at[0], targets[f])
 
-    need(2, 3)
-    last = (iota((CH, cy), 1) == cy - 1)
-    for l in range(2):
-        for q in range(8):
-            mob[q, l, cx:cx + 8, :] = jnp.zeros((8, cy), F32)
-    colf[:, :, 0:8, :] = jnp.zeros((6, 2, 8, cy), F32)
-    for c in range(cx // CH):
-        at = slice(c * CH, (c + 1) * CH)
-        props = []
-        for l in range(2):
-            v = (press[l, at], sat[0, l, at], sat[1, l, at], direc[0, l, at], direc[1, l, at], direc[2, l, at])
-            satur, dsatur, volume, m, dm = mobilities(*v)
-            rock = (1.0 + ROCK_COMP * (v[0] - 1.0)) * pore[l, at]
-            drock = ROCK_COMP * v[3] * pore[l, at]
-            mob[6, l, at, :] = v[0]
-            mob[7, l, at, :] = v[3]
-            pot = v[0] - pltpu.roll(v[0], cy - 1, 1)
-            dpot = v[3] - pltpu.roll(v[3], cy - 1, 1)
-            t = jnp.where(last, 0.0, trans[1, l, at])
-            up, dup = upwinding(pot, dpot)
-            for a in range(3):
-                mob[a, l, at, :] = m[a]
-                mob[3 + a, l, at, :] = dm[a]
-                mass = satur[a] * volume[a]
-                dmass = (dsatur[a] + COMPRESS[a] * satur[a] * v[3]) * volume[a]
-                f, df = face(
-                    t, pot, dpot, up, dup, m[a], pltpu.roll(m[a], cy - 1, 1), dm[a], pltpu.roll(dm[a], cy - 1, 1)
-                )
-                res[a, l, at, :] = rock * mass - old[a, l, at] + (f - pltpu.roll(f, 1, 1))
-                jvp[a, l, at, :] = drock * mass + rock * dmass + (df - pltpu.roll(df, 1, 1))
-            props.append((v[0], v[3], m, dm))
-        (p0, d0, m0, dm0), (p1, d1, m1, dm1) = props
-        t = trans[2, 0, at]
-        for a in range(3):
-            pot = p0 - p1 + DENSITY[a] * GRAVITY
-            dpot = d0 - d1
-            up, dup = upwinding(pot, dpot)
-            f, df = face(t, pot, dpot, up, dup, m0[a], m1[a], dm0[a], dm1[a])
-            res[a, 0, at, :] += f
-            jvp[a, 0, at, :] += df
-            res[a, 1, at, :] -= f
-            jvp[a, 1, at, :] -= df
-
-    for l in range(2):
-        for c in range(cx // CH):
-            at = slice(c * CH, (c + 1) * CH)
-            nxt = slice(c * CH + 1, (c + 1) * CH + 1)
-            here = slice(c * CH + 8, (c + 1) * CH + 8)
-            t = trans[0, l, at]
-            if c == cx // CH - 1:
-                t = jnp.where(iota((CH, cy), 0) == CH - 1, 0.0, t)
-            pot = mob[6, l, at] - mob[6, l, nxt]
-            dpot = mob[7, l, at] - mob[7, l, nxt]
-            up, dup = upwinding(pot, dpot)
-            for a in range(3):
-                f, df = face(
-                    t, pot, dpot, up, dup, mob[a, l, at], mob[a, l, nxt], mob[3 + a, l, at], mob[3 + a, l, nxt]
-                )
-                colf[a, l, here, :] = f
-                colf[3 + a, l, here, :] = df
-        for c in range(cx // CH):
-            at = slice(c * CH, (c + 1) * CH)
-            here = slice(c * CH + 8, (c + 1) * CH + 8)
-            prev = slice(c * CH + 7, (c + 1) * CH + 7)
-            for a in range(3):
-                res[a, l, at, :] += colf[a, l, here] - colf[a, l, prev]
-                jvp[a, l, at, :] += colf[3 + a, l, here] - colf[3 + a, l, prev]
-
-    need(10)
+    links, reaches = [], []
+    need(2, 3, 10)
     n_seg = perf.shape[1]
-    links, reaches = [], []
-    for i in range(share):
-        above = parent[pl.ds(gy * share + i, 1), :]
-        down = iota((n_seg, n_seg), 0)
-        link = down == above
-        reach = jnp.where(link | (down == iota((n_seg, n_seg), 1)), 1.0, 0.0).astype(BF16)
-        for _ in range((n_seg - 1).bit_length()):
-            square = jnp.dot(reach, reach, preferred_element_type=F32)
-            reach = jnp.minimum(square, 1.0).astype(BF16)
-        links.append(jnp.where(link, 1.0, 0.0).astype(BF16))
-        reaches.append(reach)
-
-    sums = part[0:3, :]
-    wait_all(rxp.at[pl.ds(1, ny - 1), pl.ds(0, 3)], r_p)
-    for k in range(1, ny):
-        sums = sums + rxp[k, 0:3, :]
-    msg2[0:3, :] = sums
-    msg2[3:4, :] = guide_part
-    for k in partners(GX_ORDER, nx):
-        to = lax.rem(gx + k, nx)
-        send(msg2.at[pl.ds(0, 4)], rx2.at[k, pl.ds(0, 4)], s_2.at[0], r_2.at[0], {"gx": to})
-
-    hots, sides = [], [[] for _ in range(6)]
-    for w in range(n_well):
-        col, row = split_cell(perf[w:w + 1, :])
-        hot = (iota((2 * cx, n_seg), 0) == col).astype(F32).astype(BF16)
-        hots += [hot, hot]
-        hit = (iota((cy, n_seg), 0) == row).astype(F32).astype(BF16).reshape(cy // 16, 16, n_seg)
-        for q in range(6):
-            for part in split2(gath[q, w:w + 1, :]):
-                wide = jnp.broadcast_to(part, (16, n_seg)).astype(BF16)
-                sides[q].append((hit * wide[None]).reshape(cy, n_seg))
-    hot = jnp.concatenate(hots, axis=1)
-    for a in range(3):
-        spread = jnp.concatenate(
-            [jnp.concatenate(sides[a], axis=1), jnp.concatenate(sides[3 + a], axis=1)], axis=0
-        )
-        out = lax.dot_general(hot, spread, NT, preferred_element_type=F32)
-        for l in range(2):
-            res[a, l] += out[l * cx:(l + 1) * cx, :cy]
-            jvp[a, l] += out[l * cx:(l + 1) * cx, cy:]
+    def exchange():
+        wait_all(rxp.at[pl.ds(1, ny - 1), pl.ds(0, 3)], r_p)
+        sums = part[0:3, :]
+        for k in range(1, ny):
+            sums = sums + rxp[k, 0:3, :]
+        msg2[0:3, :] = sums
+        for k in partners(GX_ORDER, nx):
+            to = lax.rem(gx + k, nx)
+            send(msg2.at[pl.ds(0, 3)], rx2.at[k, pl.ds(0, 3)], s_2.at[0], r_2.at[0], {"gx": to})
+
+    weave(
+        exchange,
+        spread_rates(perf, gath, split_cell, scat, cx, cy),
+        cell_terms(press, sat, old, pore, trans, direc, res, jvp, mob, colf),
+        descent(parent, gy * share, share, links, reaches),
+    )
 
     wait_all(halo_rx, r_h)
     ins, outs = [], []
@@ -383,7 +442,8 @@
             for l in range(2):
                 at = (2 * a + o) * 4 + l
                 delta = jnp.where(lane == 0, -turned[:, at:at + 1], 0.0)
-                out[a, l] += jnp.where(lane == cy - 1, turned[:, at + 2:at + 3], delta)
+                delta = jnp.where(lane == cy - 1, turned[:, at + 2:at + 3], delta)
+                out[a, l] += delta + scat[a, l * cx:(l + 1) * cx, o * cy:(o + 1) * cy]
 
     sums = msg[gy, 0:4, :]
     wait_all(rx1.at[pl.ds(1, ny - 1), pl.ds(0, 4)], r_1)
@@ -404,12 +464,10 @@
         owns.append(own)
 
     need(11, 12, 13)
-    everything = msg2[0:4, :]
-    wait_all(rx2.at[pl.ds(1, nx - 1), pl.ds(0, 4)], r_2)
+    wait_all(rxg.at[pl.ds(1, nx - 1)], r_g)
+    guide_total = guide_part
     for k in range(1, nx):
-        everything = everything + rx2[k, 0:4, :]
-    grates[...] = everything[0:3]
-    guide_total = everything[3:4]
+        guide_total = guide_total + rxg[k]
 
     wells = iota((1, n_well), 1)
     segs = iota((1, n_seg), 1)
@@ -431,9 +489,15 @@
         seg_jvp[i:i + 1, :] = jnp.where(segs == 0, root, inner)
 
     wait_all(halo_rx, s_h)
+    wait_all(rxg.at[pl.ds(1, nx - 1)], s_g)
     wait_all(rxp.at[pl.ds(1, ny - 1), pl.ds(0, 3)], s_p)
     wait_all(rx1.at[pl.ds(1, ny - 1), pl.ds(0, 4)], s_1)
-    wait_all(rx2.at[pl.ds(1, nx - 1), pl.ds(0, 4)], s_2)
+    wait_all(rx2.at[pl.ds(1, nx - 1), pl.ds(0, 3)], s_2)
+    everything = msg2[0:3, :]
+    wait_all(rx2.at[pl.ds(1, nx - 1), pl.ds(0, 3)], r_2)
+    for k in range(1, nx):
+        everything = everything + rx2[k, 0:3, :]
+    grates[...] = everything
 
 
 def write_out(*refs):
@@ -485,7 +549,10 @@
                 pltpu.VMEM((nx, 8, groups), F32),
                 pltpu.VMEM((8, groups), F32),
                 pltpu.VMEM((ny, 8, groups), F32),
-                dma((17,)), dma((1,)), dma((1,)), dma((1,)), dma((1,)), dma((1,)), dma((1,)), dma((1,)), dma((1,)),
+                pltpu.VMEM((3, 2 * cx, 2 * cy), F32),
+                pltpu.VMEM((1, groups), F32),
+                pltpu.VMEM((nx, 1, groups), F32),
+                dma((17,)), dma((1,)), dma((1,)), dma((1,)), dma((1,)), dma((1,)), dma((1,)), dma((1,)), dma((1,)), dma((1,)), dma((1,)),
             ],
             compiler_params=pltpu.CompilerParams(
                 collective_id=0, has_side_effects=True, vmem_limit_bytes=60 * 1024 * 1024

time: 23.5 us -> 21.7 us (0.923)
  Pallas kernels: 22.8 us -> 20.9 us
    pallas_call x1, Pallas kernels: 21.8 us -> 20 us  [per_device(): pl.pallas_call(lambda *refs: kernel(nx, ny, *refs), out_shape=tuple((pltp...]
where the time goes in v4:
time: 21.7 us; the launch traced here: 21.6 us
  Pallas kernels  20.9 us (96%)
  between operations  0.65 us (3%)
    pallas_call x1, Pallas kernels, per_device(): pl.pallas_call(lambda *refs: kernel(nx, ny, *refs), out_shape=tuple((pltp...  20 us
    pallas_call x1, Pallas kernels, per_device(): pl.pallas_call(write_out, out_shape=outs, in_specs=[vmem] * 5, out_specs=...  0.93 us

profile of v4, /device:TPU:1, one launch (start us, length us, event | category | flops | bytes accessed | tf_op | source)
XLA Modules:
  0.0 21.6 jit_solution(13931726447181388934)
XLA Ops:
  0.6 20.0 %newton.1 = (f32[3,2,128,128]{3,2,1,0:T(8,128)S(1)}, f32[3,2,128,128]{3,2,1,0:T(8,128)S(1)}, f32[2,128]{1,0:T(2,128)S(1)}, f32[2,128]{1,0:T(2,128)S(1)}, f32[3,128]{1,0:T(4,128)S(1)}) custom-call(f32[2,128,128]{2,1,0:T(8,128)} %refs_0_.1, f32[2,2,128,128]{3,2,1,0:T(8,128)} %refs_1_.1, f32[3,2,128,128]{3,2,1,0:T(8,128)} %refs_2_.1, f32[2,128,128]{2,1,0:T(8,128)} %refs_3_.1, ...), custom_call_target="tpu_custom_call" | custom-call | tf_op jit(solution)/shard_map/newton/pallas_call | solution.py:533
  20.6 0.9 %write_out.1 = (f32[3,2,128,128]{3,2,1,0:T(8,128)}, f32[3,2,128,128]{3,2,1,0:T(8,128)}, f32[2,128]{1,0:T(2,128)}, f32[2,128]{1,0:T(2,128)}, f32[3,128]{1,0:T(4,128)}) custom-call(f32[3,2,128,128]{3,2,1,0:T(8,128)S(1)} %get-tuple-element.10.refs_0_, f32[3,2,128,128]{3,2,1,0:T(8,128)S(1)} %get-tuple-element.11.refs_1_, ...), custom_call_target="tpu_custom_call" | custom-call | tf_op jit(solution)/shard_map/write_out/pallas_call | solution.py:562

commit v5 on v4

--- a/solution.py
+++ b/solution.py
@@ -230,7 +230,11 @@
     ) = held
     loads = [pltpu.make_async_copy(hbm[i], held[i], s_in.at[i]) for i in range(17)]
     for i in LOAD_ORDER:
-        loads[i].start()
+        if i in (0, 1, 5):
+            for j in range(hbm[i].shape[0]):
+                pltpu.make_async_copy(hbm[i].at[j], held[i].at[j], s_in.at[i]).start()
+        else:
+            loads[i].start()
     waited = set()
 
     def need(*which):
@@ -502,8 +506,12 @@
 
 def write_out(*refs):
     copies = [pltpu.make_async_copy(refs[i], refs[5 + i], refs[10].at[i]) for i in range(5)]
-    for copy in copies:
-        copy.start()
+    for i, copy in enumerate(copies):
+        if i < 2:
+            for a in range(refs[i].shape[0]):
+                pltpu.make_async_copy(refs[i].at[a], refs[5 + i].at[a], refs[10].at[i]).start()
+        else:
+            copy.start()
     for copy in copies:
         copy.wait()
 

time: 21.7 us -> 21.7 us (level)
  no operation moved by 1% of the time
where the time goes in v5:
time: 21.7 us; the launch traced here: 21.6 us
  Pallas kernels  20.9 us (96%)
  between operations  0.65 us (3%)
    pallas_call x1, Pallas kernels, per_device(): pl.pallas_call(lambda *refs: kernel(nx, ny, *refs), out_shape=tuple((pltp...  20 us
    pallas_call x1, Pallas kernels, per_device(): pl.pallas_call(write_out, out_shape=outs, in_specs=[vmem] * 5, out_specs=...  0.92 us

profile of v5, /device:TPU:1, one launch (start us, length us, event | category | flops | bytes accessed | tf_op | source)
XLA Modules:
  0.0 21.6 jit_solution(5022354576862112767)
XLA Ops:
  0.6 20.0 %newton.1 = (f32[3,2,128,128]{3,2,1,0:T(8,128)S(1)}, f32[3,2,128,128]{3,2,1,0:T(8,128)S(1)}, f32[2,128]{1,0:T(2,128)S(1)}, f32[2,128]{1,0:T(2,128)S(1)}, f32[3,128]{1,0:T(4,128)S(1)}) custom-call(f32[2,128,128]{2,1,0:T(8,128)} %refs_0_.1, f32[2,2,128,128]{3,2,1,0:T(8,128)} %refs_1_.1, f32[3,2,128,128]{3,2,1,0:T(8,128)} %refs_2_.1, f32[2,128,128]{2,1,0:T(8,128)} %refs_3_.1, ...), custom_call_target="tpu_custom_call" | custom-call | tf_op jit(solution)/shard_map/newton/pallas_call | solution.py:541
  20.6 0.9 %write_out.1 = (f32[3,2,128,128]{3,2,1,0:T(8,128)}, f32[3,2,128,128]{3,2,1,0:T(8,128)}, f32[2,128]{1,0:T(2,128)}, f32[2,128]{1,0:T(2,128)}, f32[3,128]{1,0:T(4,128)}) custom-call(f32[3,2,128,128]{3,2,1,0:T(8,128)S(1)} %get-tuple-element.10.refs_0_, f32[3,2,128,128]{3,2,1,0:T(8,128)S(1)} %get-tuple-element.11.refs_1_, ...), custom_call_target="tpu_custom_call" | custom-call | tf_op jit(solution)/shard_map/write_out/pallas_call | solution.py:570
